TPU v7x, 256 devices: a whole 4x4x8 slice. The times are simulated.
256 devices in a mesh: seq: 32 (over y, z), head: 8 (over x, core).
Axes of the slice: x: 4, y: 4, z: 8, core: 2. Of those that a mesh axis runs over, the one named last changes fastest.
Arguments:
- document_query: bfloat16 [8192, 8192], P('seq', 'head'), may hold values from -179.09903 to 179.09903
- document_key: bfloat16 [8192, 1024], P('seq', 'head'), may hold values from -6 to 6
- document_value: bfloat16 [8192, 1024], P('seq', 'head'), may hold values from -24 to 24
- branch_token_query: bfloat16 [512, 4, 8192], P('seq', None, 'head'), may hold values from -179.09903 to 179.09903
- branch_token_key: bfloat16 [512, 4, 1024], P('seq', None, 'head'), may hold values from -9 to 9
- branch_token_value: bfloat16 [512, 4, 1024], P('seq', None, 'head'), may hold values from -24 to 24
- branch_cached_key: bfloat16 [512, 128, 1024], P('seq', None, 'head'), may hold values from -9 to 9
- branch_cached_value: bfloat16 [512, 128, 1024], P('seq', None, 'head'), may hold values from -24 to 24
- suffix_length: int32 [512], P('seq'), may hold values from 1 to 128, as said below
- out_weight: bfloat16 [8192, 5120], P('head'), may hold values from -0.0625 to 0.0625
Outputs:
- prefix_out: bfloat16 [8192, 5120], P('seq', 'head')
- branch_out: bfloat16 [512, 4, 5120], P('seq', None, 'head')
Inputs may be any that keep to these rules, and one draw needn't show every extreme that they name: `suffix_length`: slots at or past a branch's length hold stale entries.
All inputs are finite; a program needn't handle non-finite values.
Results may differ from a plain program's by a relative error of at most 0.024.
Values may be sent and summed in bfloat16 or wider, within the bound.
No kernel may reach another device: no remote copies, remote signals or barrier semaphores. Data moves between devices by JAX's collectives and lax.ppermute only.
A program may use at most 128 MiB of HBM per device.

v0:
```python
import functools
import math

import jax
import jax.numpy as jnp
from jax import lax
from jax.experimental import pallas as pl
from jax.experimental.pallas import tpu as pltpu
from jax.sharding import PartitionSpec as P

HEAD_SIZE = 128
NEW_TOKENS = 4
GROUP = 8
CHUNK = 256
TILES = 10
BRANCH_ROWS = 64
NY, NZ, NX = 4, 8, 4
SCALE = HEAD_SIZE**-0.5 * math.log2(math.e)
NEG = -1e30
VMEM = pl.BlockSpec(memory_space=pltpu.VMEM)
SMEM = pl.BlockSpec(memory_space=pltpu.SMEM)
HBM = pl.BlockSpec(memory_space=pltpu.HBM)
F32 = jnp.float32
BF16 = jnp.bfloat16


def y_shift(k):
    return [(y * NZ + z, ((y + k) % NY) * NZ + z) for y in range(NY) for z in range(NZ)]


def z_shift(k):
    return [(y * NZ + z, y * NZ + (z + k) % NZ) for y in range(NY) for z in range(NZ)]


def x_shift(k):
    return [(x * 2 + c, ((x + k) % NX) * 2 + c) for x in range(NX) for c in range(2)]


def core_swap():
    return [(x * 2 + c, x * 2 + 1 - c) for x in range(NX) for c in range(2)]


def in_hbm(a):
    return pltpu.with_memory_space_constraint(a, pltpu.HBM)


def in_vmem(a):
    return pltpu.with_memory_space_constraint(a, pltpu.VMEM)


def dot_nt(a, b):
    return lax.dot_general(a, b, (((1,), (1,)), ((), ())), preferred_element_type=F32)


def dot(a, b):
    return jnp.dot(a, b, preferred_element_type=F32)


def row_peak(parts):
    cols = [p[:, i : i + 128] for p in parts for i in range(0, p.shape[1], 128)]
    return jnp.max(functools.reduce(jnp.maximum, cols), axis=1, keepdims=True)


def keys_of(chunk):
    return jnp.concatenate([chunk[:HEAD_SIZE], chunk[HEAD_SIZE : 2 * HEAD_SIZE]], axis=1)


def pack_kernel(k_ref, v_ref, o_ref):
    kt = k_ref[...].T
    o_ref[:HEAD_SIZE, :] = kt[:, :HEAD_SIZE]
    o_ref[HEAD_SIZE:CHUNK, :] = kt[:, HEAD_SIZE:]
    o_ref[CHUNK:, :] = v_ref[...]


def pack(k, v):
    return pl.pallas_call(
        pack_kernel,
        out_shape=jax.ShapeDtypeStruct((2 * CHUNK, HEAD_SIZE), BF16),
        in_specs=[VMEM] * 2,
        out_specs=VMEM,
    )(k, v)


def local_kernel(
    len_ref, dq_hbm, bq_ref, kv_ref, ck_hbm, cv_hbm, fk_ref, fv_ref,
    q_ref, acc_ref, m_ref, va_ref, ca_ref, fa_ref, dq_ref, ck_ref, cv_ref, sems
):
    copies = [
        pltpu.make_async_copy(src, dst, sems.at[i])
        for i, (src, dst) in enumerate(((dq_hbm, dq_ref), (ck_hbm, ck_ref), (cv_hbm, cv_ref)))
    ]
    for copy in copies:
        copy.start()
    copies[0].wait()
    for h in range(GROUP):
        lanes = slice(h * HEAD_SIZE, (h + 1) * HEAD_SIZE)
        q_ref[h] = dq_ref[:, lanes]
        rows = slice((h % 4) * BRANCH_ROWS, (h % 4 + 1) * BRANCH_ROWS)
        q_ref[GROUP + h // 4, rows, :] = bq_ref[:, lanes]
    va_ref[:, :HEAD_SIZE] = kv_ref[CHUNK:, :]
    va_ref[:, HEAD_SIZE:] = jnp.ones((CHUNK, HEAD_SIZE), BF16)
    fa_ref[:, :HEAD_SIZE] = fv_ref[...]
    fa_ref[:, HEAD_SIZE:] = jnp.ones((128, HEAD_SIZE), BF16)
    ca_ref[:, HEAD_SIZE:] = jnp.ones((ca_ref.shape[0], HEAD_SIZE), BF16)
    kt = keys_of(kv_ref)
    row = lax.broadcasted_iota(jnp.int32, (CHUNK, CHUNK), 0)
    col = lax.broadcasted_iota(jnp.int32, (CHUNK, CHUNK), 1)
    causal = col <= row

    def doc(t, _):
        s = jnp.where(causal, dot(q_ref[t], kt), NEG)
        m = row_peak([s]) * SCALE
        p = jnp.exp2(s * SCALE - m).astype(BF16)
        m_ref[t] = jnp.broadcast_to(m, (CHUNK, 128))
        acc_ref[t] = dot(p, va_ref[...])
        return 0

    lax.fori_loop(0, GROUP, doc, 0, unroll=4)

    copies[1].wait()
    copies[2].wait()
    ca_ref[:, :HEAD_SIZE] = cv_ref[...]
    row_branch = (row % BRANCH_ROWS) // NEW_TOKENS
    n_cached = ca_ref.shape[0] // CHUNK
    frow = lax.broadcasted_iota(jnp.int32, (CHUNK, 128), 0)
    fcol = lax.broadcasted_iota(jnp.int32, (CHUNK, 128), 1)
    same = (frow % BRANCH_ROWS) // NEW_TOKENS == fcol // NEW_TOKENS
    fresh_keep = same & (fcol % NEW_TOKENS <= frow % NEW_TOKENS)
    low = col < 128
    for t in (8, 9):
        q = q_ref[t]
        parts = [dot(q, kt)]
        for c in range(n_cached):
            s = dot_nt(q, ck_ref[c * CHUNK : (c + 1) * CHUNK, :])
            length = jnp.where(low, len_ref[2 * c], len_ref[2 * c + 1])
            owner = jnp.where(low, 2 * c, 2 * c + 1)
            keep = (row_branch == owner) & (col % 128 < length)
            parts.append(jnp.where(keep, s, NEG))
        parts.append(jnp.where(fresh_keep, dot_nt(q, fk_ref[...]), NEG))
        m = row_peak(parts) * SCALE
        m_ref[t] = jnp.broadcast_to(m, (CHUNK, 128))
        p = [jnp.exp2(s * SCALE - m).astype(BF16) for s in parts]
        total = dot(p[0], va_ref[...])
        for c in range(n_cached):
            total += dot(p[1 + c], ca_ref[c * CHUNK : (c + 1) * CHUNK, :])
        total += dot(p[-1], fa_ref[...])
        acc_ref[t] = total


def seen(place_ref, shift, rel):
    y, z = place_ref[0], place_ref[1]
    if rel:
        return ((y + rel) % NY < y).astype(jnp.int32)
    return ((z + shift) % NZ < z).astype(jnp.int32)


def accumulate(flags, q_ref, m_ref, acc_in, chunks, acc_ref, va_ref):
    ones = jnp.ones((CHUNK, HEAD_SIZE), F32)
    for c, chunk in enumerate(chunks):
        flag = (ones * flags[c].astype(F32)).astype(BF16)
        v = chunk[CHUNK:, :]
        va_ref[0, c, :, :HEAD_SIZE] = v * flag
        va_ref[0, c, :, HEAD_SIZE:] = flag
        va_ref[1, c, :, :HEAD_SIZE] = v
        va_ref[1, c, :, HEAD_SIZE:] = ones.astype(BF16)

    def tile(t, _):
        q = q_ref[t]
        m = m_ref[t]
        group = (t >= GROUP).astype(jnp.int32)
        total = acc_in[t]
        for c, chunk in enumerate(chunks):
            s = dot(q, keys_of(chunk))
            p = [
                jnp.exp2(s[:, i : i + 128] * SCALE - m).astype(BF16) for i in range(0, CHUNK, 128)
            ]
            total = total + dot(jnp.concatenate(p, axis=1), va_ref[group, c])
        acc_ref[t] = total
        return 0

    lax.fori_loop(0, TILES, tile, 0, unroll=5)


def block_kernel(first, shifts, place_ref, q_ref, m_ref, acc_in, *rest):
    srcs, (acc_ref, va_ref) = rest[:-2], rest[-2:]
    chunks = [s.at[i] for s in srcs for i in range(first, NY)]
    flags = [seen(place_ref, shift, i) for shift in shifts for i in range(first, NY)]
    accumulate(flags, q_ref, m_ref, acc_in, chunks, acc_ref, va_ref)


def block(place, q, m, acc, srcs, shifts, first, alias):
    n = sum(s.shape[0] - first for s in srcs)
    scores = TILES * CHUNK * n * CHUNK
    return pl.pallas_call(
        functools.partial(block_kernel, first, shifts),
        out_shape=pltpu.VMEM(acc.shape, F32),
        in_specs=[SMEM] + [VMEM] * (3 + len(srcs)),
        out_specs=VMEM,
        scratch_shapes=[pltpu.VMEM((2, n, CHUNK, 2 * HEAD_SIZE), BF16)],
        input_output_aliases={3: 0} if alias else {},
        compiler_params=pltpu.CompilerParams(vmem_limit_bytes=16 << 20),
        cost_estimate=pl.CostEstimate(
            flops=scores * 768, bytes_accessed=8 << 20, transcendentals=scores
        ),
    )(place, in_vmem(q), in_vmem(m), in_vmem(acc), *srcs)


def write_rows(out_ref, acc_ref):
    for t in range(GROUP):
        o = acc_ref[t, :, :HEAD_SIZE] / acc_ref[t, :, HEAD_SIZE:]
        out_ref[:CHUNK, t * 128 : (t + 1) * 128] = o.astype(BF16)
    for t in range(GROUP, TILES):
        o = (acc_ref[t, :, :HEAD_SIZE] / acc_ref[t, :, HEAD_SIZE:]).astype(BF16)
        for i in range(4):
            h = (t - GROUP) * 4 + i
            out_ref[CHUNK:, h * 128 : (h + 1) * 128] = o[i * BRANCH_ROWS : (i + 1) * BRANCH_ROWS]


def last_kernel(n_near, shifts, place_ref, q_ref, m_ref, acc_in, *rest):
    near = rest[:n_near]
    acc0_ref, weight_ref, received_ref = rest[n_near : n_near + 3]
    out_ref, mine_ref, theirs_ref, acc_ref, va_ref, run_ref, buf_ref, sem, sems = rest[-9:]
    far = rest[n_near + 3 : -9]
    width = mine_ref.shape[1] // NX
    fetches = [pltpu.make_async_copy(received_ref, theirs_ref, sems.at[NX])]
    for k in range(NX):
        chip = (place_ref[2] + k) % NX
        first = pl.multiple_of((chip * 2 + place_ref[3]) * width, 128)
        fetches.append(
            pltpu.make_async_copy(
                weight_ref.at[:, pl.ds(first, width)],
                mine_ref.at[:, pl.ds(k * width, width)],
                sems.at[k],
            )
        )
    for fetch in fetches:
        fetch.start()
    chunks = [s.at[i] for s in near for i in range(s.shape[0])]
    last_flags = [seen(place_ref, NZ // 2, i) for i in range(NY)]
    accumulate(last_flags, q_ref, m_ref, acc_in, chunks, acc_ref, va_ref)
    peak = functools.reduce(jnp.maximum, [acc_ref[t, :, HEAD_SIZE:] for t in range(TILES)])
    lowest = functools.reduce(jnp.minimum, [acc_ref[t, :, HEAD_SIZE:] for t in range(TILES)])
    fine = jnp.min(jnp.where((peak < 1e30) & (lowest > 0), 1.0, 0.0)) > 0.5

    @pl.when(fine)
    def _():
        write_rows(out_ref, acc_ref)

    @pl.when(jnp.logical_not(fine))
    def _():
        acc_ref[...] = acc0_ref[...]
        run_ref[...] = m_ref[...]

        def online(allowed):
            v = jnp.concatenate(
                [buf_ref[CHUNK:, :], jnp.ones((CHUNK, HEAD_SIZE), BF16)], axis=1
            )

            def tile(t, _):
                s = dot(q_ref[t], keys_of(buf_ref))
                old = run_ref[t]
                new = jnp.maximum(old, row_peak([s]) * SCALE)
                run_ref[t] = new
                decay = jnp.exp2(old - new)
                p = jnp.exp2(s * SCALE - new[:, :1]).astype(BF16)
                acc_ref[t] = acc_ref[t] * jnp.concatenate([decay, decay], axis=1) + dot(p, v)
                return 0

            lax.fori_loop(jnp.where(allowed == 1, 0, GROUP), TILES, tile, 0)

        for ref, shift in zip(far, shifts):
            for i in range(1 if shift == 0 else 0, NY):
                copy = pltpu.make_async_copy(ref.at[i], buf_ref, sem)
                copy.start()
                copy.wait()
                online(seen(place_ref, shift, i))
        for i, chunk in enumerate(chunks):
            buf_ref[...] = chunk[...]
            online(last_flags[i])
        write_rows(out_ref, acc_ref)

    for fetch in fetches:
        fetch.wait()


def last_block(place, q, m, acc, near, acc0, weight, received, far, shifts):
    n = sum(s.shape[0] for s in near)
    scores = TILES * CHUNK * n * CHUNK
    half = pltpu.VMEM((weight.shape[0], weight.shape[1] // 2), BF16)
    return pl.pallas_call(
        functools.partial(last_kernel, len(near), shifts),
        out_shape=[jax.ShapeDtypeStruct((CHUNK + BRANCH_ROWS, GROUP * HEAD_SIZE), BF16), half, half],
        in_specs=[SMEM]
        + [VMEM] * (4 + len(near))
        + [HBM, pl.BlockSpec(memory_space=pl.ANY)]
        + [HBM] * len(far),
        out_specs=[VMEM] * 3,
        scratch_shapes=[
            pltpu.VMEM(acc.shape, F32),
            pltpu.VMEM((2, n, CHUNK, 2 * HEAD_SIZE), BF16),
            pltpu.VMEM(m.shape, F32),
            pltpu.VMEM((2 * CHUNK, HEAD_SIZE), BF16),
            pltpu.SemaphoreType.DMA(()),
            pltpu.SemaphoreType.DMA((NX + 1,)),
        ],
        compiler_params=pltpu.CompilerParams(vmem_limit_bytes=24 << 20),
        cost_estimate=pl.CostEstimate(
            flops=scores * 768, bytes_accessed=8 << 20, transcendentals=scores
        ),
    )(
        place,
        in_vmem(q),
        in_vmem(m),
        in_vmem(acc),
        *near,
        in_vmem(acc0),
        in_hbm(weight),
        received,
        *[in_hbm(a) for a in far],
    )


def copy_kernel(place_ref, w_ref, o_ref):
    del place_ref
    o_ref[...] = w_ref[...]


def columns_for_other(weight, place, width):
    depth = weight.shape[0]
    rows = depth // 4

    def source(i, j, p):
        return j, (p[2] + i) % NX * 2 + 1 - p[3]

    return pl.pallas_call(
        copy_kernel,
        out_shape=jax.ShapeDtypeStruct((depth, NX * width), BF16),
        grid_spec=pltpu.PrefetchScalarGridSpec(
            num_scalar_prefetch=1,
            grid=(NX, 4),
            in_specs=[pl.BlockSpec((rows, width), source)],
            out_specs=pl.BlockSpec((rows, width), lambda i, j, p: (j, i)),
        ),
        compiler_params=pltpu.CompilerParams(vmem_limit_bytes=8 << 20),
        cost_estimate=pl.CostEstimate(
            flops=0, bytes_accessed=4 * depth * NX * width, transcendentals=0
        ),
    )(place, in_hbm(weight))


def own_kernel(a_ref, w_ref, o_ref):
    width = o_ref.shape[2]

    def step(k, _):
        first = pl.multiple_of(k * width, 128)
        o_ref[k] = dot(a_ref[...], w_ref[:, pl.ds(first, width)])
        return 0

    lax.fori_loop(0, NX, step, 0)


def own_products(attn, mine, width):
    rows, depth = attn.shape
    return pl.pallas_call(
        own_kernel,
        out_shape=jax.ShapeDtypeStruct((NX, rows, width), F32),
        in_specs=[VMEM] * 2,
        out_specs=VMEM,
        compiler_params=pltpu.CompilerParams(vmem_limit_bytes=16 << 20),
        cost_estimate=pl.CostEstimate(
            flops=2 * NX * rows * depth * width, bytes_accessed=0, transcendentals=0
        ),
    )(attn, in_vmem(mine))


def project_kernel(steps, own_ref, b_ref, w_ref, *out_refs):
    half, width = out_refs[0].shape
    for i, k in enumerate(steps):
        o = own_ref[k] + dot(b_ref[...], w_ref[:, k * width : (k + 1) * width])
        out_refs[2 * i][...] = o[:half].astype(BF16)
        out_refs[2 * i + 1][...] = o[half:].astype(BF16)


def project(own, other, theirs, steps):
    _, rows, width = own.shape
    half = jax.ShapeDtypeStruct((rows // 2, width), BF16)
    n = len(steps)
    return pl.pallas_call(
        functools.partial(project_kernel, steps),
        out_shape=[half] * (2 * n),
        in_specs=[VMEM] * 3,
        out_specs=[VMEM] * (2 * n),
        compiler_params=pltpu.CompilerParams(vmem_limit_bytes=20 << 20),
        cost_estimate=pl.CostEstimate(
            flops=2 * n * rows * other.shape[1] * width, bytes_accessed=0, transcendentals=0
        ),
    )(in_vmem(own), other, in_vmem(theirs))


def sum_kernel(o_ref, b0, b1, c0, c1, doc_ref, branch_ref):
    half = b0.shape[0]
    low = o_ref[:half] + b0[...].astype(F32) + c0[...].astype(F32)
    high = o_ref[half:] + b1[...].astype(F32) + c1[...].astype(F32)
    rest = CHUNK - half
    doc_ref[:half, :] = low.astype(BF16)
    doc_ref[half:, :] = high[:rest].astype(BF16)
    branch_ref[...] = high[rest:].astype(BF16)


def home_kernel(own_ref, b_ref, w_ref, o_ref):
    o_ref[...] = own_ref[0] + dot(b_ref[...], w_ref[:, : o_ref.shape[1]])


def body(
    document_query,
    document_key,
    document_value,
    branch_token_query,
    branch_token_key,
    branch_token_value,
    branch_cached_key,
    branch_cached_value,
    suffix_length,
    out_weight,
):
    seq = lax.axis_index("seq")
    head = lax.axis_index("head")
    y, z = seq // NZ, seq % NZ
    x, core = head // 2, head % 2
    width = out_weight.shape[1] // (2 * NX)

    def send(a, pairs, axis="seq"):
        return lax.ppermute(a, axis, pairs)

    def together(*a):
        return lax.optimization_barrier(a)

    place = jnp.stack([y, z, x, core]).astype(jnp.int32)
    kv = pack(document_key, document_value)
    from_down = send(kv, y_shift(1))
    from_up = send(kv, y_shift(-1))
    kv, weight = together(kv, out_weight)
    for_other = columns_for_other(weight, place, width)
    from_down, for_other = together(from_down, for_other)
    from_far = send(from_down, y_shift(1))
    column = jnp.stack([kv, from_up, from_far, from_down])
    column, kv = together(column, kv)
    right = send(column, z_shift(1))
    left = send(column, z_shift(-1))

    branch_q = branch_token_query.reshape(BRANCH_ROWS, GROUP * HEAD_SIZE)
    pad = ((0, 128 - BRANCH_ROWS), (0, 0))
    fresh_k = jnp.pad(branch_token_key.reshape(BRANCH_ROWS, HEAD_SIZE), pad)
    fresh_v = jnp.pad(branch_token_value.reshape(BRANCH_ROWS, HEAD_SIZE), pad)
    cached_k = branch_cached_key.reshape(-1, HEAD_SIZE)
    cached_v = branch_cached_value.reshape(-1, HEAD_SIZE)
    q, acc0, m = pl.pallas_call(
        local_kernel,
        out_shape=[
            pltpu.VMEM((TILES, CHUNK, HEAD_SIZE), BF16),
            pltpu.VMEM((TILES, CHUNK, 2 * HEAD_SIZE), F32),
            pltpu.VMEM((TILES, CHUNK, 128), F32),
        ],
        in_specs=[SMEM, HBM, VMEM, VMEM, HBM, HBM, VMEM, VMEM],
        out_specs=[VMEM] * 3,
        scratch_shapes=[
            pltpu.VMEM((CHUNK, 2 * HEAD_SIZE), BF16),
            pltpu.VMEM((cached_v.shape[0], 2 * HEAD_SIZE), BF16),
            pltpu.VMEM((128, 2 * HEAD_SIZE), BF16),
            pltpu.VMEM(document_query.shape, BF16),
            pltpu.VMEM(cached_k.shape, BF16),
            pltpu.VMEM(cached_v.shape, BF16),
            pltpu.SemaphoreType.DMA((3,)),
        ],
        compiler_params=pltpu.CompilerParams(vmem_limit_bytes=24 << 20),
        cost_estimate=pl.CostEstimate(
            flops=4 << 30, bytes_accessed=8 << 20, transcendentals=2 << 20
        ),
    )(
        suffix_length,
        in_hbm(document_query),
        branch_q,
        kv,
        in_hbm(cached_k),
        in_hbm(cached_v),
        fresh_k,
        fresh_v,
    )
    acc = block(place, q, m, acc0, [column], (0,), first=1, alias=False)
    far, shifts = [column], [0]

    column, for_other = together(column, for_other)
    received = send(for_other, core_swap(), "head")
    for s in (1, 2, 3):
        right, left, acc = together(right, left, acc)
        if s < 3:
            next_right = send(right, z_shift(1))
            next_left = send(left, z_shift(-1))
        else:
            next_right = send(right[:2], z_shift(1))
            next_left = send(left[2:], z_shift(-1))
        acc = block(place, q, m, acc, [right, left], (-s, s), first=0, alias=True)
        far += [right, left]
        shifts += [-s, s]
        right, left = next_right, next_left
    right, left, acc = together(right, left, acc)
    attn, mine, theirs = last_block(
        place, q, m, acc, [right, left], acc0, out_weight, received, far, tuple(shifts)
    )

    other = send(attn, core_swap(), "head")
    own = own_products(attn, mine, width)
    other, own = together(other, own)
    a0, a1 = project(own, other, theirs, (2,))
    via_up = send(a0, x_shift(1), "head")
    via_down = send(a1, x_shift(-1), "head")
    u0, u1, d0, d1 = project(own, other, theirs, (1, 3))
    high_up = send(u1, x_shift(1), "head")
    low_down = send(d0, x_shift(-1), "head")

    def add(a, b):
        return (a.astype(F32) + b.astype(F32)).astype(BF16)

    low_up = send(add(u0, via_up), x_shift(1), "head")
    high_down = send(add(d1, via_down), x_shift(-1), "head")
    home = pl.pallas_call(
        home_kernel,
        out_shape=jax.ShapeDtypeStruct(own.shape[1:], F32),
        in_specs=[VMEM] * 3,
        out_specs=VMEM,
        compiler_params=pltpu.CompilerParams(vmem_limit_bytes=20 << 20),
        cost_estimate=pl.CostEstimate(flops=1 << 29, bytes_accessed=0, transcendentals=0),
    )(own, other, theirs)
    doc_out, branch_out = pl.pallas_call(
        sum_kernel,
        out_shape=[
            jax.ShapeDtypeStruct((CHUNK, width), BF16),
            jax.ShapeDtypeStruct((BRANCH_ROWS, width), BF16),
        ],
        in_specs=[VMEM] * 5,
        out_specs=[VMEM] * 2,
        compiler_params=pltpu.CompilerParams(vmem_limit_bytes=16 << 20),
    )(home, low_up, high_up, low_down, high_down)
    return doc_out, branch_out.reshape(-1, NEW_TOKENS, width)


def solution(mesh):
    placed = (
        P("seq", "head"),
        P("seq", "head"),
        P("seq", "head"),
        P("seq", None, "head"),
        P("seq", None, "head"),
        P("seq", None, "head"),
        P("seq", None, "head"),
        P("seq", None, "head"),
        P("seq"),
        P("head", None),
    )
    return jax.shard_map(
        body,
        mesh=mesh,
        in_specs=placed,
        out_specs=(P("seq", "head"), P("seq", None, "head")),
        check_vma=False,
    )
```

profile of v0, /device:TPU:254, one launch (start us, length us, event | category | flops | bytes accessed | tf_op | source)
XLA Modules:
  0.0 291.5 jit_solution(13209003167436811537)
XLA Ops:
  0.6 1.6 shard_map.113.kv_ref
  2.2 0.2 collective-permute-start.1
  2.5 1.8 collective-permute-start
  4.3 0.1 pad_add_fusion.place_ref
  4.3 0.0 copy-start.8
  4.4 11.3 %shard_map.114 = bf16[1024,2560]{1,0:T(8,128)(2,1)} custom-call(s32[4]{0:T(128)S(1)} %pad_add_fusion.place_ref, bf16[1024,5120]{1,0:T(8,128)(2,1)} %rest_3_.1), custom_call_target="tpu_custom_call" | custom-call | bytes 10485760 | tf_op jit(solution)/shard_map/pallas_call | solution.py:335
  15.6 0.0 collective-permute-done.1
  15.6 1.4 collective-permute-start.2
  17.1 0.0 collective-permute-done
  17.1 3.5 %collective-permute-done.2 = bf16[512,128]{1,0:T(8,128)(2,1)S(1)} collective-permute-done((bf16[512,128]{1,0:T(8,128)(2,1)S(1)}, bf16[512,128]{1,0:T(8,128)(2,1)S(1)}, u32[]{:S(2)}, u32[]{:S(2)}) %collective-permute-start.2) | collective-permute-done | bytes 131104 | tf_op jit(solution)/shard_map/ppermute | solution.py:433
  20.6 0.0 copy-done.7
  20.6 0.1 pad_maximum_fusion.rest_0_.rest_5_
  20.7 0.0 copy-start
  20.7 0.1 collective-permute-start.11
  20.8 0.0 copy-done.10
  20.8 0.0 copy-done.11
  20.8 0.0 copy-done.9
  20.9 1.1 collective-permute-start.4
  22.0 2.2 collective-permute-start.3
  24.2 0.0 copy-done.8
  24.2 4.9 %shard_map.115 = (bf16[10,256,128]{2,1,0:T(8,128)(2,1)S(1)}, f32[10,256,256]{2,1,0:T(8,128)S(1)}, f32[10,256,128]{2,1,0:T(8,128)S(1)}) custom-call(s32[16]{0:T(128)S(1)} %copy-done.8, bf16[256,1024]{1,0:T(8,128)(2,1)} %dq_hbm.1, bf16[64,1024]{1,0:T(8,128)(2,1)S(1)} %reshape.22.bq_ref, bf16[512,128]{1,0:T(8,128)(2,1)S(1)} %copy-done.7, ...), custom_call_target="tpu_custom_call" | custom-call | flops 4294967296 | bytes 8388608 | tf_op jit(solution)/shard_map/pallas_call | solution.py:457
  29.1 0.0 copy-done
  29.1 3.2 %shard_map.116.acc_in = f32[10,256,256]{2,1,0:T(8,128)S(1)} custom-call(s32[4]{0:T(128)S(1)} %pad_add_fusion.place_ref, bf16[10,256,128]{2,1,0:T(8,128)(2,1)S(1)} %get-tuple-element.41.q_ref, f32[10,256,128]{2,1,0:T(8,128)S(1)} %get-tuple-element.42.m_ref, f32[10,256,256]{2,1,0:T(8,128)S(1)} %get-tuple-element.44.acc_in.rest_2_, ...), custom_call_target="tpu_custom_call" | custom-call | flops 1509949440 | bytes 8388608 | tf_op jit(solution)/shard_map/pallas_call | solution.py:194
  32.3 4.2 %collective-permute-done.4.rest_1_.rest_7_ = bf16[4,512,128]{2,1,0:T(8,128)(2,1)S(1)} collective-permute-done((bf16[4,512,128]{2,1,0:T(8,128)(2,1)S(1)}, bf16[4,512,128]{2,1,0:T(8,128)(2,1)S(1)}, u32[]{:S(2)}, u32[]{:S(2)}) %collective-permute-start.4) | collective-permute-done | bytes 524320 | tf_op jit(solution)/shard_map/ppermute | solution.py:433
  36.5 0.0 collective-permute-done.3.rest_0_.rest_6_
  36.5 3.0 %collective-permute-start.5 = (bf16[4,512,128]{2,1,0:T(8,128)(2,1)S(1)}, bf16[4,512,128]{2,1,0:T(8,128)(2,1)S(1)}, u32[]{:S(2)}, u32[]{:S(2)}) collective-permute-start(bf16[4,512,128]{2,1,0:T(8,128)(2,1)S(1)} %collective-permute-done.3.rest_0_.rest_6_), channel_id=1, source_target_pairs={{0,8},{8,16},{16,24},{24,32},{32,40},{40,48},{48,56},{56,0},{64,72... | collective-permute-start | bytes 1572872 | tf_op jit(solution)/shard_map/ppermute | solution.py:433
  39.4 0.2 collective-permute-start.6
  39.7 6.8 %shard_map.117.acc_in = f32[10,256,256]{2,1,0:T(8,128)S(1)} custom-call(s32[4]{0:T(128)S(1)} %pad_add_fusion.place_ref, bf16[10,256,128]{2,1,0:T(8,128)(2,1)S(1)} %get-tuple-element.41.q_ref, f32[10,256,128]{2,1,0:T(8,128)S(1)} %get-tuple-element.42.m_ref, f32[10,256,256]{2,1,0:T(8,128)S(1)} %shard_map.116.acc_in, ...), custom_call_target="tpu_custom_call", output_to_operand_aliasing={{}: (3, {})} | custom-call | flops 4026531840 | bytes 8388608 | tf_op jit(solution)/shard_map/pallas_call | solution.py:194
  46.5 3.6 %collective-permute-done.5.rest_0_.rest_8_ = bf16[4,512,128]{2,1,0:T(8,128)(2,1)S(1)} collective-permute-done((bf16[4,512,128]{2,1,0:T(8,128)(2,1)S(1)}, bf16[4,512,128]{2,1,0:T(8,128)(2,1)S(1)}, u32[]{:S(2)}, u32[]{:S(2)}) %collective-permute-start.5) | collective-permute-done | bytes 524320 | tf_op jit(solution)/shard_map/ppermute | solution.py:433
  50.2 3.6 %collective-permute-done.6.rest_1_.rest_9_ = bf16[4,512,128]{2,1,0:T(8,128)(2,1)S(1)} collective-permute-done((bf16[4,512,128]{2,1,0:T(8,128)(2,1)S(1)}, bf16[4,512,128]{2,1,0:T(8,128)(2,1)S(1)}, u32[]{:S(2)}, u32[]{:S(2)}) %collective-permute-start.6) | collective-permute-done | bytes 524320 | tf_op jit(solution)/shard_map/ppermute | solution.py:433
  53.8 0.1 collective-permute-start.7
  53.9 1.9 collective-permute-start.8
  55.8 6.8 %shard_map.118.acc_in = f32[10,256,256]{2,1,0:T(8,128)S(1)} custom-call(s32[4]{0:T(128)S(1)} %pad_add_fusion.place_ref, bf16[10,256,128]{2,1,0:T(8,128)(2,1)S(1)} %get-tuple-element.41.q_ref, f32[10,256,128]{2,1,0:T(8,128)S(1)} %get-tuple-element.42.m_ref, f32[10,256,256]{2,1,0:T(8,128)S(1)} %shard_map.117.acc_in, ...), custom_call_target="tpu_custom_call", output_to_operand_aliasing={{}: (3, {})} | custom-call | flops 4026531840 | bytes 8388608 | tf_op jit(solution)/shard_map/pallas_call | solution.py:194
  62.7 3.1 %collective-permute-done.7.rest_0_.rest_10_ = bf16[4,512,128]{2,1,0:T(8,128)(2,1)S(1)} collective-permute-done((bf16[4,512,128]{2,1,0:T(8,128)(2,1)S(1)}, bf16[4,512,128]{2,1,0:T(8,128)(2,1)S(1)}, u32[]{:S(2)}, u32[]{:S(2)}) %collective-permute-start.7) | collective-permute-done | bytes 524320 | tf_op jit(solution)/shard_map/ppermute | solution.py:433
  65.8 1.3 collective-permute-done.8.rest_1_.rest_11_
  67.2 0.6 collective-permute-start.10
  67.8 2.7 collective-permute-start.9
  70.5 6.8 %shard_map.119.acc_in = f32[10,256,256]{2,1,0:T(8,128)S(1)} custom-call(s32[4]{0:T(128)S(1)} %pad_add_fusion.place_ref, bf16[10,256,128]{2,1,0:T(8,128)(2,1)S(1)} %get-tuple-element.41.q_ref, f32[10,256,128]{2,1,0:T(8,128)S(1)} %get-tuple-element.42.m_ref, f32[10,256,256]{2,1,0:T(8,128)S(1)} %shard_map.118.acc_in, ...), custom_call_target="tpu_custom_call", output_to_operand_aliasing={{}: (3, {})} | custom-call | flops 4026531840 | bytes 8388608 | tf_op jit(solution)/shard_map/pallas_call | solution.py:194
  77.3 0.0 collective-permute-done.10.rest_1_
  77.3 0.0 collective-permute-done.9.rest_0_
  77.4 0.0 collective-permute-done.11.rest_4_
  77.4 190.9 %shard_map.120 = (bf16[320,1024]{1,0:T(8,128)(2,1)S(1)}, bf16[1024,2560]{1,0:T(8,128)(2,1)S(1)}, bf16[1024,2560]{1,0:T(8,128)(2,1)S(1)}) custom-call(s32[4]{0:T(128)S(1)} %pad_add_fusion.place_ref, bf16[10,256,128]{2,1,0:T(8,128)(2,1)S(1)} %get-tuple-element.41.q_ref, f32[10,256,128]{2,1,0:T(8,128)S(1)} %get-tuple-element.42.m_ref, ...), custom_call_target="tpu_custom_call" | custom-call | flops 2013265920 | bytes 8388608 | tf_op jit(solution)/shard_map/pallas_call | solution.py:290
  268.3 0.1 collective-permute-start.12
  268.4 2.7 shard_map.121.own_ref
  271.1 0.0 collective-permute-done.12.b_ref
  271.1 0.7 shard_map.124
  271.8 0.8 collective-permute-start.13
  272.6 1.5 collective-permute-start.17
  274.1 1.2 shard_map.123
  275.3 1.8 collective-permute-start.15
  277.1 0.3 collective-permute-start.16
  277.4 2.6 collective-permute-done.13
  280.0 0.1 add_convert_fusion.1
  280.0 1.8 collective-permute-start.14
  281.8 0.0 collective-permute-done.17
  281.8 0.1 add_convert_fusion
  281.9 0.4 collective-permute-start.18
  282.3 0.7 shard_map.122.o_ref
  283.0 1.4 collective-permute-done.15.b1
  284.4 1.6 collective-permute-done.16.c0
  285.9 2.4 collective-permute-done.14.b0
  288.4 1.4 collective-permute-done.18.c1
  289.8 0.8 shard_map.125
  290.6 0.7 reshape.27
  (21 shorter events, 0.1 us)
Async XLA Ops:
  2.2 13.4 %collective-permute-start.1 = (bf16[512,128]{1,0:T(8,128)(2,1)}, bf16[512,128]{1,0:T(8,128)(2,1)S(1)}, u32[]{:S(2)}, u32[]{:S(2)}) collective-permute-start(bf16[512,128]{1,0:T(8,128)(2,1)} %shard_map.113.kv_ref), channel_id=1, source_target_pairs={{0,64},{8,72},{16,80},{24,88},{32,96},{40,104},{48,112},{56,120},{... | collective-permute-start | bytes 393224 | tf_op jit(solution)/shard_map/ppermute | solution.py:433
  2.5 14.6 %collective-permute-start = (bf16[512,128]{1,0:T(8,128)(2,1)}, bf16[512,128]{1,0:T(8,128)(2,1)S(1)}, u32[]{:S(2)}, u32[]{:S(2)}) collective-permute-start(bf16[512,128]{1,0:T(8,128)(2,1)} %shard_map.113.kv_ref), channel_id=1, source_target_pairs={{0,192},{8,200},{16,208},{24,216},{32,224},{40,232},{48,240},{56,2... | collective-permute-start | bytes 393224 | tf_op jit(solution)/shard_map/ppermute | solution.py:433
  4.3 16.3 %copy-start.7 = (bf16[512,128]{1,0:T(8,128)(2,1)S(1)}, bf16[512,128]{1,0:T(8,128)(2,1)}, u32[]{:S(2)}) copy-start(bf16[512,128]{1,0:T(8,128)(2,1)} %shard_map.113.kv_ref) | copy-start | bytes 393220
  4.3 16.5 %copy-start.10 = (bf16[16,4,128]{2,1,0:T(4,128)(2,1)S(1)}, bf16[16,4,128]{2,1,0:T(4,128)(2,1)}, u32[]{:S(2)}) copy-start(bf16[16,4,128]{2,1,0:T(4,128)(2,1)} %param.14) | copy-start | bytes 49156
  4.3 16.5 %copy-start.11 = (bf16[16,4,128]{2,1,0:T(4,128)(2,1)S(1)}, bf16[16,4,128]{2,1,0:T(4,128)(2,1)}, u32[]{:S(2)}) copy-start(bf16[16,4,128]{2,1,0:T(4,128)(2,1)} %param.15) | copy-start | bytes 49156
  4.3 16.5 %copy-start.9 = (bf16[16,4,1024]{2,1,0:T(4,128)(2,1)S(1)}, bf16[16,4,1024]{2,1,0:T(4,128)(2,1)}, u32[]{:S(2)}) copy-start(bf16[16,4,1024]{2,1,0:T(4,128)(2,1)} %param.13) | copy-start | bytes 393220
  4.3 19.9 %copy-start.8 = (s32[16]{0:T(128)S(1)}, s32[16]{0:T(128)}, u32[]{:S(2)}) copy-start(s32[16]{0:T(128)} %len_ref.1) | copy-start | bytes 196
  15.6 5.0 %collective-permute-start.2 = (bf16[512,128]{1,0:T(8,128)(2,1)S(1)}, bf16[512,128]{1,0:T(8,128)(2,1)S(1)}, u32[]{:S(2)}, u32[]{:S(2)}) collective-permute-start(bf16[512,128]{1,0:T(8,128)(2,1)S(1)} %collective-permute-done.1), channel_id=1, source_target_pairs={{0,64},{8,72},{16,80},{24,88},{32,96},{40,104},{48,112},{56,120},{... | collective-permute-start | bytes 393224 | tf_op jit(solution)/shard_map/ppermute | solution.py:433
  20.7 8.4 %copy-start = (bf16[4,512,128]{2,1,0:T(8,128)(2,1)}, bf16[4,512,128]{2,1,0:T(8,128)(2,1)S(1)}, u32[]{:S(2)}) copy-start(bf16[4,512,128]{2,1,0:T(8,128)(2,1)S(1)} %pad_maximum_fusion.rest_0_.rest_5_) | copy-start | bytes 1572868
  20.7 56.7 %collective-permute-start.11 = (bf16[1024,2560]{1,0:T(8,128)(2,1)}, bf16[1024,2560]{1,0:T(8,128)(2,1)}, u32[]{:S(2)}, u32[]{:S(2)}) collective-permute-start(bf16[1024,2560]{1,0:T(8,128)(2,1)} %shard_map.114), channel_id=1, source_target_pairs={{0,1},{1,0},{2,3},{3,2},{4,5},{5,4},{6,7},{7,6},{8,9},{9,8},{10,11... | collective-permute-start | bytes 15728648 | tf_op jit(solution)/shard_map/ppermute | solution.py:433
  20.9 15.6 %collective-permute-start.4 = (bf16[4,512,128]{2,1,0:T(8,128)(2,1)S(1)}, bf16[4,512,128]{2,1,0:T(8,128)(2,1)S(1)}, u32[]{:S(2)}, u32[]{:S(2)}) collective-permute-start(bf16[4,512,128]{2,1,0:T(8,128)(2,1)S(1)} %pad_maximum_fusion.rest_0_.rest_5_), channel_id=1, source_target_pairs={{0,56},{8,0},{16,8},{24,16},{32,24},{40,32},{48,40},{56,48},{64,12... | collective-permute-start | bytes 1572872 | tf_op jit(solution)/shard_map/ppermute | solution.py:433
  22.0 14.5 %collective-permute-start.3 = (bf16[4,512,128]{2,1,0:T(8,128)(2,1)S(1)}, bf16[4,512,128]{2,1,0:T(8,128)(2,1)S(1)}, u32[]{:S(2)}, u32[]{:S(2)}) collective-permute-start(bf16[4,512,128]{2,1,0:T(8,128)(2,1)S(1)} %pad_maximum_fusion.rest_0_.rest_5_), channel_id=1, source_target_pairs={{0,8},{8,16},{16,24},{24,32},{32,40},{40,48},{48,56},{56,0},{64,72... | collective-permute-start | bytes 1572872 | tf_op jit(solution)/shard_map/ppermute | solution.py:433
  36.5 10.0 %copy-start.3 = (bf16[4,512,128]{2,1,0:T(8,128)(2,1)}, bf16[4,512,128]{2,1,0:T(8,128)(2,1)S(1)}, u32[]{:S(2)}) copy-start(bf16[4,512,128]{2,1,0:T(8,128)(2,1)S(1)} %collective-permute-done.4.rest_1_.rest_7_) | copy-start | bytes 1572868
  36.5 10.0 %copy-start.4 = (bf16[4,512,128]{2,1,0:T(8,128)(2,1)}, bf16[4,512,128]{2,1,0:T(8,128)(2,1)S(1)}, u32[]{:S(2)}) copy-start(bf16[4,512,128]{2,1,0:T(8,128)(2,1)S(1)} %collective-permute-done.3.rest_0_.rest_6_) | copy-start | bytes 1572868
  36.5 13.7 %collective-permute-start.5 = (bf16[4,512,128]{2,1,0:T(8,128)(2,1)S(1)}, bf16[4,512,128]{2,1,0:T(8,128)(2,1)S(1)}, u32[]{:S(2)}, u32[]{:S(2)}) collective-permute-start(bf16[4,512,128]{2,1,0:T(8,128)(2,1)S(1)} %collective-permute-done.3.rest_0_.rest_6_), channel_id=1, source_target_pairs={{0,8},{8,16},{16,24},{24,32},{32,40},{40,48},{48,56},{56,0},{64,72... | collective-permute-start | bytes 1572872 | tf_op jit(solution)/shard_map/ppermute | solution.py:433
  39.4 14.4 %collective-permute-start.6 = (bf16[4,512,128]{2,1,0:T(8,128)(2,1)S(1)}, bf16[4,512,128]{2,1,0:T(8,128)(2,1)S(1)}, u32[]{:S(2)}, u32[]{:S(2)}) collective-permute-start(bf16[4,512,128]{2,1,0:T(8,128)(2,1)S(1)} %collective-permute-done.4.rest_1_.rest_7_), channel_id=1, source_target_pairs={{0,56},{8,0},{16,8},{24,16},{32,24},{40,32},{48,40},{56,48},{64,12... | collective-permute-start | bytes 1572872 | tf_op jit(solution)/shard_map/ppermute | solution.py:433
  50.2 12.5 %copy-start.5 = (bf16[4,512,128]{2,1,0:T(8,128)(2,1)}, bf16[4,512,128]{2,1,0:T(8,128)(2,1)S(1)}, u32[]{:S(2)}) copy-start(bf16[4,512,128]{2,1,0:T(8,128)(2,1)S(1)} %collective-permute-done.5.rest_0_.rest_8_) | copy-start | bytes 1572868
  53.8 8.9 %copy-start.6 = (bf16[4,512,128]{2,1,0:T(8,128)(2,1)}, bf16[4,512,128]{2,1,0:T(8,128)(2,1)S(1)}, u32[]{:S(2)}) copy-start(bf16[4,512,128]{2,1,0:T(8,128)(2,1)S(1)} %collective-permute-done.6.rest_1_.rest_9_) | copy-start | bytes 1572868
  53.8 12.0 %collective-permute-start.7 = (bf16[4,512,128]{2,1,0:T(8,128)(2,1)S(1)}, bf16[4,512,128]{2,1,0:T(8,128)(2,1)S(1)}, u32[]{:S(2)}, u32[]{:S(2)}) collective-permute-start(bf16[4,512,128]{2,1,0:T(8,128)(2,1)S(1)} %collective-permute-done.5.rest_0_.rest_8_), channel_id=1, source_target_pairs={{0,8},{8,16},{16,24},{24,32},{32,40},{40,48},{48,56},{56,0},{64,72... | collective-permute-start | bytes 1572872 | tf_op jit(solution)/shard_map/ppermute | solution.py:433
  53.9 13.2 %collective-permute-start.8 = (bf16[4,512,128]{2,1,0:T(8,128)(2,1)S(1)}, bf16[4,512,128]{2,1,0:T(8,128)(2,1)S(1)}, u32[]{:S(2)}, u32[]{:S(2)}) collective-permute-start(bf16[4,512,128]{2,1,0:T(8,128)(2,1)S(1)} %collective-permute-done.6.rest_1_.rest_9_), channel_id=1, source_target_pairs={{0,56},{8,0},{16,8},{24,16},{32,24},{40,32},{48,40},{56,48},{64,12... | collective-permute-start | bytes 1572872 | tf_op jit(solution)/shard_map/ppermute | solution.py:433
  65.8 11.5 %copy-start.1 = (bf16[4,512,128]{2,1,0:T(8,128)(2,1)}, bf16[4,512,128]{2,1,0:T(8,128)(2,1)S(1)}, u32[]{:S(2)}) copy-start(bf16[4,512,128]{2,1,0:T(8,128)(2,1)S(1)} %collective-permute-done.7.rest_0_.rest_10_) | copy-start | bytes 1572868
  67.1 10.2 %copy-start.2 = (bf16[4,512,128]{2,1,0:T(8,128)(2,1)}, bf16[4,512,128]{2,1,0:T(8,128)(2,1)S(1)}, u32[]{:S(2)}) copy-start(bf16[4,512,128]{2,1,0:T(8,128)(2,1)S(1)} %collective-permute-done.8.rest_1_.rest_11_) | copy-start | bytes 1572868
  67.2 10.2 %collective-permute-start.10 = (bf16[2,512,128]{2,1,0:T(8,128)(2,1)S(1)}, bf16[2,512,128]{2,1,0:T(8,128)(2,1)S(1)}, u32[]{:S(2)}, u32[]{:S(2)}) collective-permute-start(bf16[2,512,128]{2,1,0:T(8,128)(2,1)S(1)} %slice.7), channel_id=1, source_target_pairs={{0,56},{8,0},{16,8},{24,16},{32,24},{40,32},{48,40},{56,48},{64,12... | collective-permute-start | bytes 786440 | tf_op jit(solution)/shard_map/ppermute | solution.py:433
  67.8 9.6 %collective-permute-start.9 = (bf16[2,512,128]{2,1,0:T(8,128)(2,1)S(1)}, bf16[2,512,128]{2,1,0:T(8,128)(2,1)S(1)}, u32[]{:S(2)}, u32[]{:S(2)}) collective-permute-start(bf16[2,512,128]{2,1,0:T(8,128)(2,1)S(1)} %slice.6), channel_id=1, source_target_pairs={{0,8},{8,16},{16,24},{24,32},{32,40},{40,48},{48,56},{56,0},{64,72... | collective-permute-start | bytes 786440 | tf_op jit(solution)/shard_map/ppermute | solution.py:433
  268.3 2.8 collective-permute-start.12
  271.8 8.2 %collective-permute-start.13 = (bf16[160,640]{1,0:T(8,128)(2,1)S(1)}, bf16[160,640]{1,0:T(8,128)(2,1)S(1)}, u32[]{:S(2)}, u32[]{:S(2)}) collective-permute-start(bf16[160,640]{1,0:T(8,128)(2,1)S(1)} %get-tuple-element.65), channel_id=1, source_target_pairs={{0,2},{1,3},{2,4},{3,5},{4,6},{5,7},{6,0},{7,1},{8,10},{9,11},{10,... | collective-permute-start | bytes 614408 | tf_op jit(solution)/shard_map/ppermute | solution.py:433
  272.6 9.2 %collective-permute-start.17 = (bf16[160,640]{1,0:T(8,128)(2,1)S(1)}, bf16[160,640]{1,0:T(8,128)(2,1)S(1)}, u32[]{:S(2)}, u32[]{:S(2)}) collective-permute-start(bf16[160,640]{1,0:T(8,128)(2,1)S(1)} %get-tuple-element.69), channel_id=1, source_target_pairs={{0,6},{1,7},{2,0},{3,1},{4,2},{5,3},{6,4},{7,5},{8,14},{9,15},{10,... | collective-permute-start | bytes 614408 | tf_op jit(solution)/shard_map/ppermute | solution.py:433
  275.3 9.0 %collective-permute-start.15 = (bf16[160,640]{1,0:T(8,128)(2,1)S(1)}, bf16[160,640]{1,0:T(8,128)(2,1)S(1)}, u32[]{:S(2)}, u32[]{:S(2)}) collective-permute-start(bf16[160,640]{1,0:T(8,128)(2,1)S(1)} %get-tuple-element.66), channel_id=1, source_target_pairs={{0,2},{1,3},{2,4},{3,5},{4,6},{5,7},{6,0},{7,1},{8,10},{9,11},{10,... | collective-permute-start | bytes 614408 | tf_op jit(solution)/shard_map/ppermute | solution.py:433
  277.1 8.8 %collective-permute-start.16 = (bf16[160,640]{1,0:T(8,128)(2,1)S(1)}, bf16[160,640]{1,0:T(8,128)(2,1)S(1)}, u32[]{:S(2)}, u32[]{:S(2)}) collective-permute-start(bf16[160,640]{1,0:T(8,128)(2,1)S(1)} %get-tuple-element.67), channel_id=1, source_target_pairs={{0,6},{1,7},{2,0},{3,1},{4,2},{5,3},{6,4},{7,5},{8,14},{9,15},{10,... | collective-permute-start | bytes 614408 | tf_op jit(solution)/shard_map/ppermute | solution.py:433
  280.0 8.3 %collective-permute-start.14 = (bf16[160,640]{1,0:T(8,128)(2,1)S(1)}, bf16[160,640]{1,0:T(8,128)(2,1)S(1)}, u32[]{:S(2)}, u32[]{:S(2)}) collective-permute-start(bf16[160,640]{1,0:T(8,128)(2,1)S(1)} %add_convert_fusion.1), channel_id=1, source_target_pairs={{0,2},{1,3},{2,4},{3,5},{4,6},{5,7},{6,0},{7,1},{8,10},{9,11},{10,... | collective-permute-start | bytes 614408 | tf_op jit(solution)/shard_map/ppermute | solution.py:433
  281.9 7.9 %collective-permute-start.18 = (bf16[160,640]{1,0:T(8,128)(2,1)S(1)}, bf16[160,640]{1,0:T(8,128)(2,1)S(1)}, u32[]{:S(2)}, u32[]{:S(2)}) collective-permute-start(bf16[160,640]{1,0:T(8,128)(2,1)S(1)} %add_convert_fusion), channel_id=1, source_target_pairs={{0,6},{1,7},{2,0},{3,1},{4,2},{5,3},{6,4},{7,5},{8,14},{9,15},{10,... | collective-permute-start | bytes 614408 | tf_op jit(solution)/shard_map/ppermute | solution.py:433
where the time goes:
time: 295 us; the launch traced here: 291 us
  Pallas kernels  238 us (81%)
  waiting for transfers between devices  28.8 us (10%)
  starting transfers between devices  22.1 us (7%)
    pallas_call x1, Pallas kernels, last_block(): pl.pallas_call(functools.partial(last_kernel, len(near), shifts), out_sha...  191 us
    ppermute x19, waiting for transfers between devices, send(): return lax.ppermute(a, axis, pairs)  28.8 us
    pallas_call x4, Pallas kernels, block(): pl.pallas_call(functools.partial(block_kernel, first, shifts), out_shape=...  23.6 us
    ppermute x19, starting transfers between devices, send(): return lax.ppermute(a, axis, pairs)  22.1 us
    pallas_call x1, Pallas kernels, columns_for_other(): pl.pallas_call(copy_kernel, out_shape=jax.ShapeDtypeStruct((depth, NX * w...  11.3 us
  transfers between devices with their start and end apart: 19, of which 11 were waited for; matrix products, arithmetic and copies ran while one was open for 0% of the time, Pallas kernels for 15%

commit v1 on v0

--- a/solution.py
+++ b/solution.py
@@ -320,30 +320,33 @@
     )
 
 
-def copy_kernel(place_ref, w_ref, o_ref):
-    del place_ref
-    o_ref[...] = w_ref[...]
-
-
-def columns_for_other(weight, place, width):
-    depth = weight.shape[0]
-    rows = depth // 4
-
-    def source(i, j, p):
-        return j, (p[2] + i) % NX * 2 + 1 - p[3]
-
+def columns_kernel(place_ref, w_ref, o_ref, sems):
+    width = o_ref.shape[1] // NX
+    copies = []
+    for k in range(NX):
+        chip = (place_ref[2] + k) % NX
+        first = pl.multiple_of((chip * 2 + 1 - place_ref[3]) * width, 128)
+        copies.append(
+            pltpu.make_async_copy(
+                w_ref.at[:, pl.ds(first, width)], o_ref.at[:, pl.ds(k * width, width)], sems.at[k]
+            )
+        )
+    for copy in copies:
+        copy.start()
+    for copy in copies:
+        copy.wait()
+
+
+def columns_for_other(weight, place):
     return pl.pallas_call(
-        copy_kernel,
-        out_shape=jax.ShapeDtypeStruct((depth, NX * width), BF16),
-        grid_spec=pltpu.PrefetchScalarGridSpec(
-            num_scalar_prefetch=1,
-            grid=(NX, 4),
-            in_specs=[pl.BlockSpec((rows, width), source)],
-            out_specs=pl.BlockSpec((rows, width), lambda i, j, p: (j, i)),
-        ),
+        columns_kernel,
+        out_shape=pltpu.VMEM((weight.shape[0], weight.shape[1] // 2), BF16),
+        in_specs=[SMEM, HBM],
+        out_specs=VMEM,
+        scratch_shapes=[pltpu.SemaphoreType.DMA((NX,))],
         compiler_params=pltpu.CompilerParams(vmem_limit_bytes=8 << 20),
         cost_estimate=pl.CostEstimate(
-            flops=0, bytes_accessed=4 * depth * NX * width, transcendentals=0
+            flops=0, bytes_accessed=2 * weight.size, transcendentals=0
         ),
     )(place, in_hbm(weight))
 
@@ -440,7 +443,7 @@
     from_down = send(kv, y_shift(1))
     from_up = send(kv, y_shift(-1))
     kv, weight = together(kv, out_weight)
-    for_other = columns_for_other(weight, place, width)
+    for_other = columns_for_other(weight, place)
     from_down, for_other = together(from_down, for_other)
     from_far = send(from_down, y_shift(1))
     column = jnp.stack([kv, from_up, from_far, from_down])
@@ -489,7 +492,7 @@
     acc = block(place, q, m, acc0, [column], (0,), first=1, alias=False)
     far, shifts = [column], [0]
 
-    column, for_other = together(column, for_other)
+    acc, for_other = together(acc, for_other)
     received = send(for_other, core_swap(), "head")
     for s in (1, 2, 3):
         right, left, acc = together(right, left, acc)

time: 295 us -> 298 us (1.010)
  waiting for transfers between devices: 28.8 us -> 36.7 us
  Pallas kernels: 238 us -> 231 us
    pallas_call x1, Pallas kernels: 11.3 us -> 3.11 us  [columns_for_other(): pl.pallas_call(columns_kernel, out_shape=pltpu.VMEM((weight.shape[0], wei...]
    ppermute x19, waiting for transfers between devices: 28.8 us -> 36.7 us  [send(): return lax.ppermute(a, axis, pairs)]
  transfers between devices with their start and end apart: 19 -> 19, of which waited for: 11 -> 11; matrix products, arithmetic and copies ran while one was open for 0% -> 0% of each run, Pallas kernels for 15% -> 10%
where the time goes in v1:
time: 298 us; the launch traced here: 294 us
  Pallas kernels  231 us (78%)
  waiting for transfers between devices  36.7 us (12%)
  starting transfers between devices  22.1 us (7%)
  local copies, waits for them, and re-layouts  3.1 us (1%)
    pallas_call x1, Pallas kernels, last_block(): pl.pallas_call(functools.partial(last_kernel, len(near), shifts), out_sha...  191 us
    ppermute x19, waiting for transfers between devices, send(): return lax.ppermute(a, axis, pairs)  36.7 us
    pallas_call x4, Pallas kernels, block(): pl.pallas_call(functools.partial(block_kernel, first, shifts), out_shape=...  23.6 us
    ppermute x19, starting transfers between devices, send(): return lax.ppermute(a, axis, pairs)  22.1 us
  transfers between devices with their start and end apart: 19, of which 11 were waited for; matrix products, arithmetic and copies ran while one was open for 0% of the time, Pallas kernels for 10%

profile of v1, /device:TPU:254, one launch (start us, length us, event | category | flops | bytes accessed | tf_op | source)
XLA Modules:
  0.0 294.4 jit_solution(15088028351655419673)
XLA Ops:
  0.6 1.6 shard_map.113.kv_ref
  2.2 0.2 collective-permute-start.1
  2.5 1.8 collective-permute-start
  4.3 0.1 pad_add_fusion.place_ref
  4.3 0.0 copy-start.9
  4.4 3.1 %shard_map.114 = bf16[1024,2560]{1,0:T(8,128)(2,1)S(1)} custom-call(s32[4]{0:T(128)S(1)} %pad_add_fusion.place_ref, bf16[1024,5120]{1,0:T(8,128)(2,1)} %rest_3_.1), custom_call_target="tpu_custom_call" | custom-call | bytes 10485760 | tf_op jit(solution)/shard_map/pallas_call | solution.py:341
  7.5 0.0 copy-start
  7.5 2.3 copy-done
  9.8 0.0 collective-permute-done.1
  9.8 1.4 collective-permute-start.2
  11.2 0.0 copy-done.11
  11.2 0.0 copy-done.12
  11.3 0.0 copy-done.10
  11.3 0.0 collective-permute-done
  11.3 3.4 %collective-permute-done.2 = bf16[512,128]{1,0:T(8,128)(2,1)S(1)} collective-permute-done((bf16[512,128]{1,0:T(8,128)(2,1)S(1)}, bf16[512,128]{1,0:T(8,128)(2,1)S(1)}, u32[]{:S(2)}, u32[]{:S(2)}) %collective-permute-start.2) | collective-permute-done | bytes 131104 | tf_op jit(solution)/shard_map/ppermute | solution.py:436
  14.8 0.1 pad_maximum_fusion.rest_0_.rest_5_
  14.9 0.0 slice-start.1
  14.9 5.4 %shard_map.115 = (bf16[10,256,128]{2,1,0:T(8,128)(2,1)S(1)}, f32[10,256,256]{2,1,0:T(8,128)S(1)}, f32[10,256,128]{2,1,0:T(8,128)S(1)}) custom-call(s32[16]{0:T(128)S(1)} %copy-done.9, bf16[256,1024]{1,0:T(8,128)(2,1)} %dq_hbm.1, bf16[64,1024]{1,0:T(8,128)(2,1)S(1)} %reshape.22.bq_ref, bf16[512,128]{1,0:T(8,128)(2,1)S(1)} %copy-done.8, ...), custom_call_target="tpu_custom_call" | custom-call | flops 4294967296 | bytes 8388608 | tf_op jit(solution)/shard_map/pallas_call | solution.py:460
  20.2 3.2 %shard_map.116.acc_in = f32[10,256,256]{2,1,0:T(8,128)S(1)} custom-call(s32[4]{0:T(128)S(1)} %pad_add_fusion.place_ref, bf16[10,256,128]{2,1,0:T(8,128)(2,1)S(1)} %get-tuple-element.42.q_ref, f32[10,256,128]{2,1,0:T(8,128)S(1)} %get-tuple-element.43.m_ref, f32[10,256,256]{2,1,0:T(8,128)S(1)} %get-tuple-element.45.acc_in.rest_2_, ...), custom_call_target="tpu_custom_call" | custom-call | flops 1509949440 | bytes 8388608 | tf_op jit(solution)/shard_map/pallas_call | solution.py:194
  23.5 0.1 collective-permute-start.11
  23.6 1.1 collective-permute-start.4
  24.7 0.0 copy-done.1
  24.7 2.2 collective-permute-start.3
  26.9 12.2 %collective-permute-done.4.rest_1_.rest_7_ = bf16[4,512,128]{2,1,0:T(8,128)(2,1)S(1)} collective-permute-done((bf16[4,512,128]{2,1,0:T(8,128)(2,1)S(1)}, bf16[4,512,128]{2,1,0:T(8,128)(2,1)S(1)}, u32[]{:S(2)}, u32[]{:S(2)}) %collective-permute-start.4) | collective-permute-done | bytes 524320 | tf_op jit(solution)/shard_map/ppermute | solution.py:436
  39.1 0.0 collective-permute-done.3.rest_0_.rest_6_
  39.1 3.0 %collective-permute-start.5 = (bf16[4,512,128]{2,1,0:T(8,128)(2,1)S(1)}, bf16[4,512,128]{2,1,0:T(8,128)(2,1)S(1)}, u32[]{:S(2)}, u32[]{:S(2)}) collective-permute-start(bf16[4,512,128]{2,1,0:T(8,128)(2,1)S(1)} %collective-permute-done.3.rest_0_.rest_6_), channel_id=1, source_target_pairs={{0,8},{8,16},{16,24},{24,32},{32,40},{40,48},{48,56},{56,0},{64,72... | collective-permute-start | bytes 1572872 | tf_op jit(solution)/shard_map/ppermute | solution.py:436
  42.1 0.2 collective-permute-start.6
  42.4 6.8 %shard_map.117.acc_in = f32[10,256,256]{2,1,0:T(8,128)S(1)} custom-call(s32[4]{0:T(128)S(1)} %pad_add_fusion.place_ref, bf16[10,256,128]{2,1,0:T(8,128)(2,1)S(1)} %get-tuple-element.42.q_ref, f32[10,256,128]{2,1,0:T(8,128)S(1)} %get-tuple-element.43.m_ref, f32[10,256,256]{2,1,0:T(8,128)S(1)} %shard_map.116.acc_in, ...), custom_call_target="tpu_custom_call", output_to_operand_aliasing={{}: (3, {})} | custom-call | flops 4026531840 | bytes 8388608 | tf_op jit(solution)/shard_map/pallas_call | solution.py:194
  49.2 3.6 %collective-permute-done.5.rest_0_.rest_8_ = bf16[4,512,128]{2,1,0:T(8,128)(2,1)S(1)} collective-permute-done((bf16[4,512,128]{2,1,0:T(8,128)(2,1)S(1)}, bf16[4,512,128]{2,1,0:T(8,128)(2,1)S(1)}, u32[]{:S(2)}, u32[]{:S(2)}) %collective-permute-start.5) | collective-permute-done | bytes 524320 | tf_op jit(solution)/shard_map/ppermute | solution.py:436
  52.8 3.6 %collective-permute-done.6.rest_1_.rest_9_ = bf16[4,512,128]{2,1,0:T(8,128)(2,1)S(1)} collective-permute-done((bf16[4,512,128]{2,1,0:T(8,128)(2,1)S(1)}, bf16[4,512,128]{2,1,0:T(8,128)(2,1)S(1)}, u32[]{:S(2)}, u32[]{:S(2)}) %collective-permute-start.6) | collective-permute-done | bytes 524320 | tf_op jit(solution)/shard_map/ppermute | solution.py:436
  56.4 0.1 collective-permute-start.7
  56.5 1.9 collective-permute-start.8
  58.5 6.8 %shard_map.118.acc_in = f32[10,256,256]{2,1,0:T(8,128)S(1)} custom-call(s32[4]{0:T(128)S(1)} %pad_add_fusion.place_ref, bf16[10,256,128]{2,1,0:T(8,128)(2,1)S(1)} %get-tuple-element.42.q_ref, f32[10,256,128]{2,1,0:T(8,128)S(1)} %get-tuple-element.43.m_ref, f32[10,256,256]{2,1,0:T(8,128)S(1)} %shard_map.117.acc_in, ...), custom_call_target="tpu_custom_call", output_to_operand_aliasing={{}: (3, {})} | custom-call | flops 4026531840 | bytes 8388608 | tf_op jit(solution)/shard_map/pallas_call | solution.py:194
  65.3 3.1 %collective-permute-done.7.rest_0_.rest_10_ = bf16[4,512,128]{2,1,0:T(8,128)(2,1)S(1)} collective-permute-done((bf16[4,512,128]{2,1,0:T(8,128)(2,1)S(1)}, bf16[4,512,128]{2,1,0:T(8,128)(2,1)S(1)}, u32[]{:S(2)}, u32[]{:S(2)}) %collective-permute-start.7) | collective-permute-done | bytes 524320 | tf_op jit(solution)/shard_map/ppermute | solution.py:436
  68.4 1.3 collective-permute-done.8.rest_1_.rest_11_
  69.8 0.6 collective-permute-start.10
  70.4 2.7 collective-permute-start.9
  73.1 6.8 %shard_map.119.acc_in = f32[10,256,256]{2,1,0:T(8,128)S(1)} custom-call(s32[4]{0:T(128)S(1)} %pad_add_fusion.place_ref, bf16[10,256,128]{2,1,0:T(8,128)(2,1)S(1)} %get-tuple-element.42.q_ref, f32[10,256,128]{2,1,0:T(8,128)S(1)} %get-tuple-element.43.m_ref, f32[10,256,256]{2,1,0:T(8,128)S(1)} %shard_map.118.acc_in, ...), custom_call_target="tpu_custom_call", output_to_operand_aliasing={{}: (3, {})} | custom-call | flops 4026531840 | bytes 8388608 | tf_op jit(solution)/shard_map/pallas_call | solution.py:194
  79.9 0.0 collective-permute-done.10.rest_1_
  79.9 0.0 collective-permute-done.9.rest_0_
  79.9 0.0 collective-permute-done.11.rest_4_
  79.9 191.3 %shard_map.120 = (bf16[320,1024]{1,0:T(8,128)(2,1)S(1)}, bf16[1024,2560]{1,0:T(8,128)(2,1)S(1)}, bf16[1024,2560]{1,0:T(8,128)(2,1)S(1)}) custom-call(s32[4]{0:T(128)S(1)} %pad_add_fusion.place_ref, bf16[10,256,128]{2,1,0:T(8,128)(2,1)S(1)} %get-tuple-element.42.q_ref, f32[10,256,128]{2,1,0:T(8,128)S(1)} %get-tuple-element.43.m_ref, ...), custom_call_target="tpu_custom_call" | custom-call | flops 2013265920 | bytes 8388608 | tf_op jit(solution)/shard_map/pallas_call | solution.py:290
  271.2 0.1 collective-permute-start.12
  271.3 2.7 shard_map.121.own_ref
  274.1 0.0 collective-permute-done.12.b_ref
  274.1 0.7 shard_map.124
  274.8 0.8 collective-permute-start.13
  275.5 1.5 collective-permute-start.17
  277.1 1.2 shard_map.123
  278.3 1.8 collective-permute-start.15
  280.0 0.3 collective-permute-start.16
  280.4 2.6 collective-permute-done.13
  282.9 0.1 add_convert_fusion.1
  283.0 1.8 collective-permute-start.14
  284.7 0.0 collective-permute-done.17
  284.7 0.1 add_convert_fusion
  284.8 0.4 collective-permute-start.18
  285.2 0.7 shard_map.122.o_ref
  285.9 1.4 collective-permute-done.15.b1
  287.3 1.6 collective-permute-done.16.c0
  288.9 2.4 collective-permute-done.14.b0
  291.3 1.4 collective-permute-done.18.c1
  292.7 0.8 shard_map.125
  293.5 0.7 reshape.27
  (28 shorter events, 0.1 us)
Async XLA Ops:
  2.2 7.6 %collective-permute-start.1 = (bf16[512,128]{1,0:T(8,128)(2,1)}, bf16[512,128]{1,0:T(8,128)(2,1)S(1)}, u32[]{:S(2)}, u32[]{:S(2)}) collective-permute-start(bf16[512,128]{1,0:T(8,128)(2,1)} %shard_map.113.kv_ref), channel_id=1, source_target_pairs={{0,64},{8,72},{16,80},{24,88},{32,96},{40,104},{48,112},{56,120},{... | collective-permute-start | bytes 393224 | tf_op jit(solution)/shard_map/ppermute | solution.py:436
  2.5 8.9 %collective-permute-start = (bf16[512,128]{1,0:T(8,128)(2,1)}, bf16[512,128]{1,0:T(8,128)(2,1)S(1)}, u32[]{:S(2)}, u32[]{:S(2)}) collective-permute-start(bf16[512,128]{1,0:T(8,128)(2,1)} %shard_map.113.kv_ref), channel_id=1, source_target_pairs={{0,192},{8,200},{16,208},{24,216},{32,224},{40,232},{48,240},{56,2... | collective-permute-start | bytes 393224 | tf_op jit(solution)/shard_map/ppermute | solution.py:436
  4.3 6.9 %copy-start.11 = (bf16[16,4,128]{2,1,0:T(4,128)(2,1)S(1)}, bf16[16,4,128]{2,1,0:T(4,128)(2,1)}, u32[]{:S(2)}) copy-start(bf16[16,4,128]{2,1,0:T(4,128)(2,1)} %param.14) | copy-start | bytes 49156
  4.3 6.9 %copy-start.12 = (bf16[16,4,128]{2,1,0:T(4,128)(2,1)S(1)}, bf16[16,4,128]{2,1,0:T(4,128)(2,1)}, u32[]{:S(2)}) copy-start(bf16[16,4,128]{2,1,0:T(4,128)(2,1)} %param.15) | copy-start | bytes 49156
  4.3 6.9 %copy-start.10 = (bf16[16,4,1024]{2,1,0:T(4,128)(2,1)S(1)}, bf16[16,4,1024]{2,1,0:T(4,128)(2,1)}, u32[]{:S(2)}) copy-start(bf16[16,4,1024]{2,1,0:T(4,128)(2,1)} %param.13) | copy-start | bytes 393220
  4.3 10.4 %copy-start.8 = (bf16[512,128]{1,0:T(8,128)(2,1)S(1)}, bf16[512,128]{1,0:T(8,128)(2,1)}, u32[]{:S(2)}) copy-start(bf16[512,128]{1,0:T(8,128)(2,1)} %shard_map.113.kv_ref) | copy-start | bytes 393220
  4.3 10.5 %copy-start.9 = (s32[16]{0:T(128)S(1)}, s32[16]{0:T(128)}, u32[]{:S(2)}) copy-start(s32[16]{0:T(128)} %len_ref.1) | copy-start | bytes 196
  7.5 2.3 copy-start
  9.8 5.0 %collective-permute-start.2 = (bf16[512,128]{1,0:T(8,128)(2,1)S(1)}, bf16[512,128]{1,0:T(8,128)(2,1)S(1)}, u32[]{:S(2)}, u32[]{:S(2)}) collective-permute-start(bf16[512,128]{1,0:T(8,128)(2,1)S(1)} %collective-permute-done.1), channel_id=1, source_target_pairs={{0,64},{8,72},{16,80},{24,88},{32,96},{40,104},{48,112},{56,120},{... | collective-permute-start | bytes 393224 | tf_op jit(solution)/shard_map/ppermute | solution.py:436
  14.8 8.7 %slice-start = ((s8[5242880]{0:T(1024)(128)(4,1)}), s8[4194304]{0:T(1024)(128)(4,1)S(1)}, s32[]{:S(2)}) async-start(s8[5242880]{0:T(1024)(128)(4,1)} %bitcast.12), calls=%async_computation | async-start | bytes 8388608
  14.8 9.8 %copy-start.1 = (bf16[4,512,128]{2,1,0:T(8,128)(2,1)}, bf16[4,512,128]{2,1,0:T(8,128)(2,1)S(1)}, u32[]{:S(2)}) copy-start(bf16[4,512,128]{2,1,0:T(8,128)(2,1)S(1)} %pad_maximum_fusion.rest_0_.rest_5_) | copy-start | bytes 1572868
  14.9 8.6 %slice-start.1 = ((s8[5242880]{0:T(1024)(128)(4,1)}), s8[1048576]{0:T(1024)(128)(4,1)S(1)}, s32[]{:S(2)}) async-start(s8[5242880]{0:T(1024)(128)(4,1)} %bitcast.12), calls=%async_computation.1 | async-start | bytes 2097152
  23.5 56.4 %collective-permute-start.11 = (bf16[1024,2560]{1,0:T(8,128)(2,1)S(1)}, bf16[1024,2560]{1,0:T(8,128)(2,1)S(1)}, u32[]{:S(2)}, u32[]{:S(2)}) collective-permute-start(bf16[1024,2560]{1,0:T(8,128)(2,1)S(1)} %bitcast.13), channel_id=1, source_target_pairs={{0,1},{1,0},{2,3},{3,2},{4,5},{5,4},{6,7},{7,6},{8,9},{9,8},{10,11... | collective-permute-start | bytes 15728648 | tf_op jit(solution)/shard_map/ppermute | solution.py:436
  23.6 15.6 %collective-permute-start.4 = (bf16[4,512,128]{2,1,0:T(8,128)(2,1)S(1)}, bf16[4,512,128]{2,1,0:T(8,128)(2,1)S(1)}, u32[]{:S(2)}, u32[]{:S(2)}) collective-permute-start(bf16[4,512,128]{2,1,0:T(8,128)(2,1)S(1)} %pad_maximum_fusion.rest_0_.rest_5_), channel_id=1, source_target_pairs={{0,56},{8,0},{16,8},{24,16},{32,24},{40,32},{48,40},{56,48},{64,12... | collective-permute-start | bytes 1572872 | tf_op jit(solution)/shard_map/ppermute | solution.py:436
  24.7 14.5 %collective-permute-start.3 = (bf16[4,512,128]{2,1,0:T(8,128)(2,1)S(1)}, bf16[4,512,128]{2,1,0:T(8,128)(2,1)S(1)}, u32[]{:S(2)}, u32[]{:S(2)}) collective-permute-start(bf16[4,512,128]{2,1,0:T(8,128)(2,1)S(1)} %pad_maximum_fusion.rest_0_.rest_5_), channel_id=1, source_target_pairs={{0,8},{8,16},{16,24},{24,32},{32,40},{40,48},{48,56},{56,0},{64,72... | collective-permute-start | bytes 1572872 | tf_op jit(solution)/shard_map/ppermute | solution.py:436
  39.1 10.0 %copy-start.4 = (bf16[4,512,128]{2,1,0:T(8,128)(2,1)}, bf16[4,512,128]{2,1,0:T(8,128)(2,1)S(1)}, u32[]{:S(2)}) copy-start(bf16[4,512,128]{2,1,0:T(8,128)(2,1)S(1)} %collective-permute-done.4.rest_1_.rest_7_) | copy-start | bytes 1572868
  39.1 10.0 %copy-start.5 = (bf16[4,512,128]{2,1,0:T(8,128)(2,1)}, bf16[4,512,128]{2,1,0:T(8,128)(2,1)S(1)}, u32[]{:S(2)}) copy-start(bf16[4,512,128]{2,1,0:T(8,128)(2,1)S(1)} %collective-permute-done.3.rest_0_.rest_6_) | copy-start | bytes 1572868
  39.1 13.6 %collective-permute-start.5 = (bf16[4,512,128]{2,1,0:T(8,128)(2,1)S(1)}, bf16[4,512,128]{2,1,0:T(8,128)(2,1)S(1)}, u32[]{:S(2)}, u32[]{:S(2)}) collective-permute-start(bf16[4,512,128]{2,1,0:T(8,128)(2,1)S(1)} %collective-permute-done.3.rest_0_.rest_6_), channel_id=1, source_target_pairs={{0,8},{8,16},{16,24},{24,32},{32,40},{40,48},{48,56},{56,0},{64,72... | collective-permute-start | bytes 1572872 | tf_op jit(solution)/shard_map/ppermute | solution.py:436
  42.1 14.3 %collective-permute-start.6 = (bf16[4,512,128]{2,1,0:T(8,128)(2,1)S(1)}, bf16[4,512,128]{2,1,0:T(8,128)(2,1)S(1)}, u32[]{:S(2)}, u32[]{:S(2)}) collective-permute-start(bf16[4,512,128]{2,1,0:T(8,128)(2,1)S(1)} %collective-permute-done.4.rest_1_.rest_7_), channel_id=1, source_target_pairs={{0,56},{8,0},{16,8},{24,16},{32,24},{40,32},{48,40},{56,48},{64,12... | collective-permute-start | bytes 1572872 | tf_op jit(solution)/shard_map/ppermute | solution.py:436
  52.8 12.5 %copy-start.6 = (bf16[4,512,128]{2,1,0:T(8,128)(2,1)}, bf16[4,512,128]{2,1,0:T(8,128)(2,1)S(1)}, u32[]{:S(2)}) copy-start(bf16[4,512,128]{2,1,0:T(8,128)(2,1)S(1)} %collective-permute-done.5.rest_0_.rest_8_) | copy-start | bytes 1572868
  56.4 8.9 %copy-start.7 = (bf16[4,512,128]{2,1,0:T(8,128)(2,1)}, bf16[4,512,128]{2,1,0:T(8,128)(2,1)S(1)}, u32[]{:S(2)}) copy-start(bf16[4,512,128]{2,1,0:T(8,128)(2,1)S(1)} %collective-permute-done.6.rest_1_.rest_9_) | copy-start | bytes 1572868
  56.4 12.0 %collective-permute-start.7 = (bf16[4,512,128]{2,1,0:T(8,128)(2,1)S(1)}, bf16[4,512,128]{2,1,0:T(8,128)(2,1)S(1)}, u32[]{:S(2)}, u32[]{:S(2)}) collective-permute-start(bf16[4,512,128]{2,1,0:T(8,128)(2,1)S(1)} %collective-permute-done.5.rest_0_.rest_8_), channel_id=1, source_target_pairs={{0,8},{8,16},{16,24},{24,32},{32,40},{40,48},{48,56},{56,0},{64,72... | collective-permute-start | bytes 1572872 | tf_op jit(solution)/shard_map/ppermute | solution.py:436
  56.5 13.2 %collective-permute-start.8 = (bf16[4,512,128]{2,1,0:T(8,128)(2,1)S(1)}, bf16[4,512,128]{2,1,0:T(8,128)(2,1)S(1)}, u32[]{:S(2)}, u32[]{:S(2)}) collective-permute-start(bf16[4,512,128]{2,1,0:T(8,128)(2,1)S(1)} %collective-permute-done.6.rest_1_.rest_9_), channel_id=1, source_target_pairs={{0,56},{8,0},{16,8},{24,16},{32,24},{40,32},{48,40},{56,48},{64,12... | collective-permute-start | bytes 1572872 | tf_op jit(solution)/shard_map/ppermute | solution.py:436
  68.4 11.5 %copy-start.2 = (bf16[4,512,128]{2,1,0:T(8,128)(2,1)}, bf16[4,512,128]{2,1,0:T(8,128)(2,1)S(1)}, u32[]{:S(2)}) copy-start(bf16[4,512,128]{2,1,0:T(8,128)(2,1)S(1)} %collective-permute-done.7.rest_0_.rest_10_) | copy-start | bytes 1572868
  69.7 10.2 %copy-start.3 = (bf16[4,512,128]{2,1,0:T(8,128)(2,1)}, bf16[4,512,128]{2,1,0:T(8,128)(2,1)S(1)}, u32[]{:S(2)}) copy-start(bf16[4,512,128]{2,1,0:T(8,128)(2,1)S(1)} %collective-permute-done.8.rest_1_.rest_11_) | copy-start | bytes 1572868
  69.8 10.2 %collective-permute-start.10 = (bf16[2,512,128]{2,1,0:T(8,128)(2,1)S(1)}, bf16[2,512,128]{2,1,0:T(8,128)(2,1)S(1)}, u32[]{:S(2)}, u32[]{:S(2)}) collective-permute-start(bf16[2,512,128]{2,1,0:T(8,128)(2,1)S(1)} %slice.7), channel_id=1, source_target_pairs={{0,56},{8,0},{16,8},{24,16},{32,24},{40,32},{48,40},{56,48},{64,12... | collective-permute-start | bytes 786440 | tf_op jit(solution)/shard_map/ppermute | solution.py:436
  70.4 9.5 %collective-permute-start.9 = (bf16[2,512,128]{2,1,0:T(8,128)(2,1)S(1)}, bf16[2,512,128]{2,1,0:T(8,128)(2,1)S(1)}, u32[]{:S(2)}, u32[]{:S(2)}) collective-permute-start(bf16[2,512,128]{2,1,0:T(8,128)(2,1)S(1)} %slice.6), channel_id=1, source_target_pairs={{0,8},{8,16},{16,24},{24,32},{32,40},{40,48},{48,56},{56,0},{64,72... | collective-permute-start | bytes 786440 | tf_op jit(solution)/shard_map/ppermute | solution.py:436
  271.2 2.8 collective-permute-start.12
  274.8 8.2 %collective-permute-start.13 = (bf16[160,640]{1,0:T(8,128)(2,1)S(1)}, bf16[160,640]{1,0:T(8,128)(2,1)S(1)}, u32[]{:S(2)}, u32[]{:S(2)}) collective-permute-start(bf16[160,640]{1,0:T(8,128)(2,1)S(1)} %get-tuple-element.67), channel_id=1, source_target_pairs={{0,2},{1,3},{2,4},{3,5},{4,6},{5,7},{6,0},{7,1},{8,10},{9,11},{10,... | collective-permute-start | bytes 614408 | tf_op jit(solution)/shard_map/ppermute | solution.py:436
  275.5 9.2 %collective-permute-start.17 = (bf16[160,640]{1,0:T(8,128)(2,1)S(1)}, bf16[160,640]{1,0:T(8,128)(2,1)S(1)}, u32[]{:S(2)}, u32[]{:S(2)}) collective-permute-start(bf16[160,640]{1,0:T(8,128)(2,1)S(1)} %get-tuple-element.71), channel_id=1, source_target_pairs={{0,6},{1,7},{2,0},{3,1},{4,2},{5,3},{6,4},{7,5},{8,14},{9,15},{10,... | collective-permute-start | bytes 614408 | tf_op jit(solution)/shard_map/ppermute | solution.py:436
  278.3 9.0 %collective-permute-start.15 = (bf16[160,640]{1,0:T(8,128)(2,1)S(1)}, bf16[160,640]{1,0:T(8,128)(2,1)S(1)}, u32[]{:S(2)}, u32[]{:S(2)}) collective-permute-start(bf16[160,640]{1,0:T(8,128)(2,1)S(1)} %get-tuple-element.68), channel_id=1, source_target_pairs={{0,2},{1,3},{2,4},{3,5},{4,6},{5,7},{6,0},{7,1},{8,10},{9,11},{10,... | collective-permute-start | bytes 614408 | tf_op jit(solution)/shard_map/ppermute | solution.py:436
  280.0 8.8 %collective-permute-start.16 = (bf16[160,640]{1,0:T(8,128)(2,1)S(1)}, bf16[160,640]{1,0:T(8,128)(2,1)S(1)}, u32[]{:S(2)}, u32[]{:S(2)}) collective-permute-start(bf16[160,640]{1,0:T(8,128)(2,1)S(1)} %get-tuple-element.69), channel_id=1, source_target_pairs={{0,6},{1,7},{2,0},{3,1},{4,2},{5,3},{6,4},{7,5},{8,14},{9,15},{10,... | collective-permute-start | bytes 614408 | tf_op jit(solution)/shard_map/ppermute | solution.py:436
  283.0 8.3 %collective-permute-start.14 = (bf16[160,640]{1,0:T(8,128)(2,1)S(1)}, bf16[160,640]{1,0:T(8,128)(2,1)S(1)}, u32[]{:S(2)}, u32[]{:S(2)}) collective-permute-start(bf16[160,640]{1,0:T(8,128)(2,1)S(1)} %add_convert_fusion.1), channel_id=1, source_target_pairs={{0,2},{1,3},{2,4},{3,5},{4,6},{5,7},{6,0},{7,1},{8,10},{9,11},{10,... | collective-permute-start | bytes 614408 | tf_op jit(solution)/shard_map/ppermute | solution.py:436
  284.8 7.9 %collective-permute-start.18 = (bf16[160,640]{1,0:T(8,128)(2,1)S(1)}, bf16[160,640]{1,0:T(8,128)(2,1)S(1)}, u32[]{:S(2)}, u32[]{:S(2)}) collective-permute-start(bf16[160,640]{1,0:T(8,128)(2,1)S(1)} %add_convert_fusion), channel_id=1, source_target_pairs={{0,6},{1,7},{2,0},{3,1},{4,2},{5,3},{6,4},{7,5},{8,14},{9,15},{10,... | collective-permute-start | bytes 614408 | tf_op jit(solution)/shard_map/ppermute | solution.py:436

commit v2 on v1

--- a/solution.py
+++ b/solution.py
@@ -446,6 +446,8 @@
     for_other = columns_for_other(weight, place)
     from_down, for_other = together(from_down, for_other)
     from_far = send(from_down, y_shift(1))
+    from_up, for_other = together(from_up, for_other)
+    received = send(for_other, core_swap(), "head")
     column = jnp.stack([kv, from_up, from_far, from_down])
     column, kv = together(column, kv)
     right = send(column, z_shift(1))
@@ -492,8 +494,6 @@
     acc = block(place, q, m, acc0, [column], (0,), first=1, alias=False)
     far, shifts = [column], [0]
 
-    acc, for_other = together(acc, for_other)
-    received = send(for_other, core_swap(), "head")
     for s in (1, 2, 3):
         right, left, acc = together(right, left, acc)
         if s < 3:

time: 298 us -> 287 us (0.963)
  waiting for transfers between devices: 36.7 us -> 27 us
    ppermute x19, waiting for transfers between devices: 36.7 us -> 27 us  [send(): return lax.ppermute(a, axis, pairs)]
  transfers between devices with their start and end apart: 19 -> 19, of which waited for: 11 -> 11; matrix products, arithmetic and copies ran while one was open for 0% -> 0% of each run, Pallas kernels for 10% -> 14%
where the time goes in v2:
time: 287 us; the launch traced here: 284 us
  Pallas kernels  233 us (81%)
  waiting for transfers between devices  27 us (9%)
  starting transfers between devices  22.2 us (8%)
    pallas_call x1, Pallas kernels, last_block(): pl.pallas_call(functools.partial(last_kernel, len(near), shifts), out_sha...  191 us
    ppermute x19, waiting for transfers between devices, send(): return lax.ppermute(a, axis, pairs)  27 us
    pallas_call x4, Pallas kernels, block(): pl.pallas_call(functools.partial(block_kernel, first, shifts), out_shape=...  23.6 us
    ppermute x19, starting transfers between devices, send(): return lax.ppermute(a, axis, pairs)  22.2 us
  transfers between devices with their start and end apart: 19, of which 11 were waited for; matrix products, arithmetic and copies ran while one was open for 0% of the time, Pallas kernels for 14%

profile of v2, /device:TPU:254, one launch (start us, length us, event | category | flops | bytes accessed | tf_op | source)
XLA Modules:
  0.0 283.9 jit_solution(15555384487276811033)
XLA Ops:
  0.6 1.6 shard_map.113.kv_ref
  2.2 0.2 collective-permute-start.1
  2.5 1.8 collective-permute-start
  4.3 0.1 pad_add_fusion.place_ref
  4.3 0.0 copy-start.8
  4.4 5.5 %shard_map.114 = bf16[1024,2560]{1,0:T(8,128)(2,1)} custom-call(s32[4]{0:T(128)S(1)} %pad_add_fusion.place_ref, bf16[1024,5120]{1,0:T(8,128)(2,1)} %rest_3_.1), custom_call_target="tpu_custom_call" | custom-call | bytes 10485760 | tf_op jit(solution)/shard_map/pallas_call | solution.py:341
  9.8 0.0 collective-permute-done.1
  9.8 0.0 collective-permute-done
  9.8 0.1 collective-permute-start.11
  9.9 1.5 collective-permute-start.2
  11.4 0.0 copy-done.10
  11.5 0.0 copy-done.11
  11.5 0.0 copy-done.9
  11.5 4.3 %collective-permute-done.2 = bf16[512,128]{1,0:T(8,128)(2,1)S(1)} collective-permute-done((bf16[512,128]{1,0:T(8,128)(2,1)S(1)}, bf16[512,128]{1,0:T(8,128)(2,1)S(1)}, u32[]{:S(2)}, u32[]{:S(2)}) %collective-permute-start.2) | collective-permute-done | bytes 131104 | tf_op jit(solution)/shard_map/ppermute | solution.py:436
  15.8 0.0 copy-done.7
  15.9 0.1 pad_maximum_fusion.rest_0_.rest_5_
  15.9 0.0 copy-start
  15.9 1.1 collective-permute-start.4
  17.0 2.2 collective-permute-start.3
  19.2 0.0 copy-done.8
  19.2 4.9 %shard_map.115 = (bf16[10,256,128]{2,1,0:T(8,128)(2,1)S(1)}, f32[10,256,256]{2,1,0:T(8,128)S(1)}, f32[10,256,128]{2,1,0:T(8,128)S(1)}) custom-call(s32[16]{0:T(128)S(1)} %copy-done.8, bf16[256,1024]{1,0:T(8,128)(2,1)} %dq_hbm.1, bf16[64,1024]{1,0:T(8,128)(2,1)S(1)} %reshape.22.bq_ref, bf16[512,128]{1,0:T(8,128)(2,1)S(1)} %copy-done.7, ...), custom_call_target="tpu_custom_call" | custom-call | flops 4294967296 | bytes 8388608 | tf_op jit(solution)/shard_map/pallas_call | solution.py:462
  24.1 0.0 copy-done
  24.1 3.2 %shard_map.116.acc_in = f32[10,256,256]{2,1,0:T(8,128)S(1)} custom-call(s32[4]{0:T(128)S(1)} %pad_add_fusion.place_ref, bf16[10,256,128]{2,1,0:T(8,128)(2,1)S(1)} %get-tuple-element.44.q_ref, f32[10,256,128]{2,1,0:T(8,128)S(1)} %get-tuple-element.45.m_ref, f32[10,256,256]{2,1,0:T(8,128)S(1)} %get-tuple-element.47.acc_in.rest_2_, ...), custom_call_target="tpu_custom_call" | custom-call | flops 1509949440 | bytes 8388608 | tf_op jit(solution)/shard_map/pallas_call | solution.py:194
  27.3 3.3 %collective-permute-done.4.rest_1_.rest_7_ = bf16[4,512,128]{2,1,0:T(8,128)(2,1)S(1)} collective-permute-done((bf16[4,512,128]{2,1,0:T(8,128)(2,1)S(1)}, bf16[4,512,128]{2,1,0:T(8,128)(2,1)S(1)}, u32[]{:S(2)}, u32[]{:S(2)}) %collective-permute-start.4) | collective-permute-done | bytes 524320 | tf_op jit(solution)/shard_map/ppermute | solution.py:436
  30.7 0.0 collective-permute-done.3.rest_0_.rest_6_
  30.7 3.0 %collective-permute-start.5 = (bf16[4,512,128]{2,1,0:T(8,128)(2,1)S(1)}, bf16[4,512,128]{2,1,0:T(8,128)(2,1)S(1)}, u32[]{:S(2)}, u32[]{:S(2)}) collective-permute-start(bf16[4,512,128]{2,1,0:T(8,128)(2,1)S(1)} %collective-permute-done.3.rest_0_.rest_6_), channel_id=1, source_target_pairs={{0,8},{8,16},{16,24},{24,32},{32,40},{40,48},{48,56},{56,0},{64,72... | collective-permute-start | bytes 1572872 | tf_op jit(solution)/shard_map/ppermute | solution.py:436
  33.7 0.2 collective-permute-start.6
  33.9 6.8 %shard_map.117.acc_in = f32[10,256,256]{2,1,0:T(8,128)S(1)} custom-call(s32[4]{0:T(128)S(1)} %pad_add_fusion.place_ref, bf16[10,256,128]{2,1,0:T(8,128)(2,1)S(1)} %get-tuple-element.44.q_ref, f32[10,256,128]{2,1,0:T(8,128)S(1)} %get-tuple-element.45.m_ref, f32[10,256,256]{2,1,0:T(8,128)S(1)} %shard_map.116.acc_in, ...), custom_call_target="tpu_custom_call", output_to_operand_aliasing={{}: (3, {})} | custom-call | flops 4026531840 | bytes 8388608 | tf_op jit(solution)/shard_map/pallas_call | solution.py:194
  40.7 2.7 collective-permute-done.5.rest_0_.rest_8_
  43.4 3.6 %collective-permute-done.6.rest_1_.rest_9_ = bf16[4,512,128]{2,1,0:T(8,128)(2,1)S(1)} collective-permute-done((bf16[4,512,128]{2,1,0:T(8,128)(2,1)S(1)}, bf16[4,512,128]{2,1,0:T(8,128)(2,1)S(1)}, u32[]{:S(2)}, u32[]{:S(2)}) %collective-permute-start.6) | collective-permute-done | bytes 524320 | tf_op jit(solution)/shard_map/ppermute | solution.py:436
  47.1 0.1 collective-permute-start.7
  47.2 1.9 collective-permute-start.8
  49.1 6.8 %shard_map.118.acc_in = f32[10,256,256]{2,1,0:T(8,128)S(1)} custom-call(s32[4]{0:T(128)S(1)} %pad_add_fusion.place_ref, bf16[10,256,128]{2,1,0:T(8,128)(2,1)S(1)} %get-tuple-element.44.q_ref, f32[10,256,128]{2,1,0:T(8,128)S(1)} %get-tuple-element.45.m_ref, f32[10,256,256]{2,1,0:T(8,128)S(1)} %shard_map.117.acc_in, ...), custom_call_target="tpu_custom_call", output_to_operand_aliasing={{}: (3, {})} | custom-call | flops 4026531840 | bytes 8388608 | tf_op jit(solution)/shard_map/pallas_call | solution.py:194
  56.0 2.2 collective-permute-done.7.rest_0_.rest_10_
  58.2 1.3 collective-permute-done.8.rest_1_.rest_11_
  59.5 1.5 collective-permute-start.10
  61.1 1.8 collective-permute-start.9
  62.9 6.8 %shard_map.119.acc_in = f32[10,256,256]{2,1,0:T(8,128)S(1)} custom-call(s32[4]{0:T(128)S(1)} %pad_add_fusion.place_ref, bf16[10,256,128]{2,1,0:T(8,128)(2,1)S(1)} %get-tuple-element.44.q_ref, f32[10,256,128]{2,1,0:T(8,128)S(1)} %get-tuple-element.45.m_ref, f32[10,256,256]{2,1,0:T(8,128)S(1)} %shard_map.118.acc_in, ...), custom_call_target="tpu_custom_call", output_to_operand_aliasing={{}: (3, {})} | custom-call | flops 4026531840 | bytes 8388608 | tf_op jit(solution)/shard_map/pallas_call | solution.py:194
  69.7 0.0 collective-permute-done.10.rest_1_
  69.7 0.0 collective-permute-done.9.rest_0_
  69.7 0.0 collective-permute-done.11.rest_4_
  69.7 190.9 %shard_map.120 = (bf16[320,1024]{1,0:T(8,128)(2,1)S(1)}, bf16[1024,2560]{1,0:T(8,128)(2,1)S(1)}, bf16[1024,2560]{1,0:T(8,128)(2,1)S(1)}) custom-call(s32[4]{0:T(128)S(1)} %pad_add_fusion.place_ref, bf16[10,256,128]{2,1,0:T(8,128)(2,1)S(1)} %get-tuple-element.44.q_ref, f32[10,256,128]{2,1,0:T(8,128)S(1)} %get-tuple-element.45.m_ref, ...), custom_call_target="tpu_custom_call" | custom-call | flops 2013265920 | bytes 8388608 | tf_op jit(solution)/shard_map/pallas_call | solution.py:290
  260.7 0.1 collective-permute-start.12
  260.8 2.7 shard_map.121.own_ref
  263.5 0.0 collective-permute-done.12.b_ref
  263.5 0.7 shard_map.124
  264.2 0.8 collective-permute-start.13
  265.0 1.5 collective-permute-start.17
  266.5 1.2 shard_map.123
  267.7 1.8 collective-permute-start.15
  269.5 0.3 collective-permute-start.16
  269.8 2.6 collective-permute-done.13
  272.3 0.1 add_convert_fusion.1
  272.4 1.8 collective-permute-start.14
  274.2 0.0 collective-permute-done.17
  274.2 0.1 add_convert_fusion
  274.2 0.4 collective-permute-start.18
  274.6 0.7 shard_map.122.o_ref
  275.3 1.4 collective-permute-done.15.b1
  276.7 1.6 collective-permute-done.16.c0
  278.3 2.4 collective-permute-done.14.b0
  280.7 1.4 collective-permute-done.18.c1
  282.1 0.8 shard_map.125
  283.0 0.7 reshape.27
  (21 shorter events, 0.1 us)
Async XLA Ops:
  2.2 7.6 %collective-permute-start.1 = (bf16[512,128]{1,0:T(8,128)(2,1)}, bf16[512,128]{1,0:T(8,128)(2,1)S(1)}, u32[]{:S(2)}, u32[]{:S(2)}) collective-permute-start(bf16[512,128]{1,0:T(8,128)(2,1)} %shard_map.113.kv_ref), channel_id=1, source_target_pairs={{0,64},{8,72},{16,80},{24,88},{32,96},{40,104},{48,112},{56,120},{... | collective-permute-start | bytes 393224 | tf_op jit(solution)/shard_map/ppermute | solution.py:436
  2.5 7.4 %collective-permute-start = (bf16[512,128]{1,0:T(8,128)(2,1)}, bf16[512,128]{1,0:T(8,128)(2,1)S(1)}, u32[]{:S(2)}, u32[]{:S(2)}) collective-permute-start(bf16[512,128]{1,0:T(8,128)(2,1)} %shard_map.113.kv_ref), channel_id=1, source_target_pairs={{0,192},{8,200},{16,208},{24,216},{32,224},{40,232},{48,240},{56,2... | collective-permute-start | bytes 393224 | tf_op jit(solution)/shard_map/ppermute | solution.py:436
  4.3 7.1 %copy-start.10 = (bf16[16,4,128]{2,1,0:T(4,128)(2,1)S(1)}, bf16[16,4,128]{2,1,0:T(4,128)(2,1)}, u32[]{:S(2)}) copy-start(bf16[16,4,128]{2,1,0:T(4,128)(2,1)} %param.14) | copy-start | bytes 49156
  4.3 7.1 %copy-start.11 = (bf16[16,4,128]{2,1,0:T(4,128)(2,1)S(1)}, bf16[16,4,128]{2,1,0:T(4,128)(2,1)}, u32[]{:S(2)}) copy-start(bf16[16,4,128]{2,1,0:T(4,128)(2,1)} %param.15) | copy-start | bytes 49156
  4.3 7.1 %copy-start.9 = (bf16[16,4,1024]{2,1,0:T(4,128)(2,1)S(1)}, bf16[16,4,1024]{2,1,0:T(4,128)(2,1)}, u32[]{:S(2)}) copy-start(bf16[16,4,1024]{2,1,0:T(4,128)(2,1)} %param.13) | copy-start | bytes 393220
  4.3 11.5 %copy-start.7 = (bf16[512,128]{1,0:T(8,128)(2,1)S(1)}, bf16[512,128]{1,0:T(8,128)(2,1)}, u32[]{:S(2)}) copy-start(bf16[512,128]{1,0:T(8,128)(2,1)} %shard_map.113.kv_ref) | copy-start | bytes 393220
  4.3 14.9 %copy-start.8 = (s32[16]{0:T(128)S(1)}, s32[16]{0:T(128)}, u32[]{:S(2)}) copy-start(s32[16]{0:T(128)} %len_ref.1) | copy-start | bytes 196
  9.8 59.9 %collective-permute-start.11 = (bf16[1024,2560]{1,0:T(8,128)(2,1)}, bf16[1024,2560]{1,0:T(8,128)(2,1)}, u32[]{:S(2)}, u32[]{:S(2)}) collective-permute-start(bf16[1024,2560]{1,0:T(8,128)(2,1)} %shard_map.114), channel_id=1, source_target_pairs={{0,1},{1,0},{2,3},{3,2},{4,5},{5,4},{6,7},{7,6},{8,9},{9,8},{10,11... | collective-permute-start | bytes 15728648 | tf_op jit(solution)/shard_map/ppermute | solution.py:436
  9.9 5.9 %collective-permute-start.2 = (bf16[512,128]{1,0:T(8,128)(2,1)S(1)}, bf16[512,128]{1,0:T(8,128)(2,1)S(1)}, u32[]{:S(2)}, u32[]{:S(2)}) collective-permute-start(bf16[512,128]{1,0:T(8,128)(2,1)S(1)} %collective-permute-done.1), channel_id=1, source_target_pairs={{0,64},{8,72},{16,80},{24,88},{32,96},{40,104},{48,112},{56,120},{... | collective-permute-start | bytes 393224 | tf_op jit(solution)/shard_map/ppermute | solution.py:436
  15.9 8.2 %copy-start = (bf16[4,512,128]{2,1,0:T(8,128)(2,1)}, bf16[4,512,128]{2,1,0:T(8,128)(2,1)S(1)}, u32[]{:S(2)}) copy-start(bf16[4,512,128]{2,1,0:T(8,128)(2,1)S(1)} %pad_maximum_fusion.rest_0_.rest_5_) | copy-start | bytes 1572868
  15.9 14.8 %collective-permute-start.4 = (bf16[4,512,128]{2,1,0:T(8,128)(2,1)S(1)}, bf16[4,512,128]{2,1,0:T(8,128)(2,1)S(1)}, u32[]{:S(2)}, u32[]{:S(2)}) collective-permute-start(bf16[4,512,128]{2,1,0:T(8,128)(2,1)S(1)} %pad_maximum_fusion.rest_0_.rest_5_), channel_id=1, source_target_pairs={{0,56},{8,0},{16,8},{24,16},{32,24},{40,32},{48,40},{56,48},{64,12... | collective-permute-start | bytes 1572872 | tf_op jit(solution)/shard_map/ppermute | solution.py:436
  17.0 13.7 %collective-permute-start.3 = (bf16[4,512,128]{2,1,0:T(8,128)(2,1)S(1)}, bf16[4,512,128]{2,1,0:T(8,128)(2,1)S(1)}, u32[]{:S(2)}, u32[]{:S(2)}) collective-permute-start(bf16[4,512,128]{2,1,0:T(8,128)(2,1)S(1)} %pad_maximum_fusion.rest_0_.rest_5_), channel_id=1, source_target_pairs={{0,8},{8,16},{16,24},{24,32},{32,40},{40,48},{48,56},{56,0},{64,72... | collective-permute-start | bytes 1572872 | tf_op jit(solution)/shard_map/ppermute | solution.py:436
  30.7 10.0 %copy-start.3 = (bf16[4,512,128]{2,1,0:T(8,128)(2,1)}, bf16[4,512,128]{2,1,0:T(8,128)(2,1)S(1)}, u32[]{:S(2)}) copy-start(bf16[4,512,128]{2,1,0:T(8,128)(2,1)S(1)} %collective-permute-done.4.rest_1_.rest_7_) | copy-start | bytes 1572868
  30.7 10.0 %copy-start.4 = (bf16[4,512,128]{2,1,0:T(8,128)(2,1)}, bf16[4,512,128]{2,1,0:T(8,128)(2,1)S(1)}, u32[]{:S(2)}) copy-start(bf16[4,512,128]{2,1,0:T(8,128)(2,1)S(1)} %collective-permute-done.3.rest_0_.rest_6_) | copy-start | bytes 1572868
  30.7 12.7 %collective-permute-start.5 = (bf16[4,512,128]{2,1,0:T(8,128)(2,1)S(1)}, bf16[4,512,128]{2,1,0:T(8,128)(2,1)S(1)}, u32[]{:S(2)}, u32[]{:S(2)}) collective-permute-start(bf16[4,512,128]{2,1,0:T(8,128)(2,1)S(1)} %collective-permute-done.3.rest_0_.rest_6_), channel_id=1, source_target_pairs={{0,8},{8,16},{16,24},{24,32},{32,40},{40,48},{48,56},{56,0},{64,72... | collective-permute-start | bytes 1572872 | tf_op jit(solution)/shard_map/ppermute | solution.py:436
  33.7 13.4 %collective-permute-start.6 = (bf16[4,512,128]{2,1,0:T(8,128)(2,1)S(1)}, bf16[4,512,128]{2,1,0:T(8,128)(2,1)S(1)}, u32[]{:S(2)}, u32[]{:S(2)}) collective-permute-start(bf16[4,512,128]{2,1,0:T(8,128)(2,1)S(1)} %collective-permute-done.4.rest_1_.rest_7_), channel_id=1, source_target_pairs={{0,56},{8,0},{16,8},{24,16},{32,24},{40,32},{48,40},{56,48},{64,12... | collective-permute-start | bytes 1572872 | tf_op jit(solution)/shard_map/ppermute | solution.py:436
  43.4 12.5 %copy-start.5 = (bf16[4,512,128]{2,1,0:T(8,128)(2,1)}, bf16[4,512,128]{2,1,0:T(8,128)(2,1)S(1)}, u32[]{:S(2)}) copy-start(bf16[4,512,128]{2,1,0:T(8,128)(2,1)S(1)} %collective-permute-done.5.rest_0_.rest_8_) | copy-start | bytes 1572868
  47.1 8.9 %copy-start.6 = (bf16[4,512,128]{2,1,0:T(8,128)(2,1)}, bf16[4,512,128]{2,1,0:T(8,128)(2,1)S(1)}, u32[]{:S(2)}) copy-start(bf16[4,512,128]{2,1,0:T(8,128)(2,1)S(1)} %collective-permute-done.6.rest_1_.rest_9_) | copy-start | bytes 1572868
  47.1 11.1 %collective-permute-start.7 = (bf16[4,512,128]{2,1,0:T(8,128)(2,1)S(1)}, bf16[4,512,128]{2,1,0:T(8,128)(2,1)S(1)}, u32[]{:S(2)}, u32[]{:S(2)}) collective-permute-start(bf16[4,512,128]{2,1,0:T(8,128)(2,1)S(1)} %collective-permute-done.5.rest_0_.rest_8_), channel_id=1, source_target_pairs={{0,8},{8,16},{16,24},{24,32},{32,40},{40,48},{48,56},{56,0},{64,72... | collective-permute-start | bytes 1572872 | tf_op jit(solution)/shard_map/ppermute | solution.py:436
  47.2 12.3 %collective-permute-start.8 = (bf16[4,512,128]{2,1,0:T(8,128)(2,1)S(1)}, bf16[4,512,128]{2,1,0:T(8,128)(2,1)S(1)}, u32[]{:S(2)}, u32[]{:S(2)}) collective-permute-start(bf16[4,512,128]{2,1,0:T(8,128)(2,1)S(1)} %collective-permute-done.6.rest_1_.rest_9_), channel_id=1, source_target_pairs={{0,56},{8,0},{16,8},{24,16},{32,24},{40,32},{48,40},{56,48},{64,12... | collective-permute-start | bytes 1572872 | tf_op jit(solution)/shard_map/ppermute | solution.py:436
  58.2 11.5 %copy-start.1 = (bf16[4,512,128]{2,1,0:T(8,128)(2,1)}, bf16[4,512,128]{2,1,0:T(8,128)(2,1)S(1)}, u32[]{:S(2)}) copy-start(bf16[4,512,128]{2,1,0:T(8,128)(2,1)S(1)} %collective-permute-done.7.rest_0_.rest_10_) | copy-start | bytes 1572868
  59.5 10.2 %copy-start.2 = (bf16[4,512,128]{2,1,0:T(8,128)(2,1)}, bf16[4,512,128]{2,1,0:T(8,128)(2,1)S(1)}, u32[]{:S(2)}) copy-start(bf16[4,512,128]{2,1,0:T(8,128)(2,1)S(1)} %collective-permute-done.8.rest_1_.rest_11_) | copy-start | bytes 1572868
  59.5 10.2 %collective-permute-start.10 = (bf16[2,512,128]{2,1,0:T(8,128)(2,1)S(1)}, bf16[2,512,128]{2,1,0:T(8,128)(2,1)S(1)}, u32[]{:S(2)}, u32[]{:S(2)}) collective-permute-start(bf16[2,512,128]{2,1,0:T(8,128)(2,1)S(1)} %slice.7), channel_id=1, source_target_pairs={{0,56},{8,0},{16,8},{24,16},{32,24},{40,32},{48,40},{56,48},{64,12... | collective-permute-start | bytes 786440 | tf_op jit(solution)/shard_map/ppermute | solution.py:436
  61.1 8.7 %collective-permute-start.9 = (bf16[2,512,128]{2,1,0:T(8,128)(2,1)S(1)}, bf16[2,512,128]{2,1,0:T(8,128)(2,1)S(1)}, u32[]{:S(2)}, u32[]{:S(2)}) collective-permute-start(bf16[2,512,128]{2,1,0:T(8,128)(2,1)S(1)} %slice.6), channel_id=1, source_target_pairs={{0,8},{8,16},{16,24},{24,32},{32,40},{40,48},{48,56},{56,0},{64,72... | collective-permute-start | bytes 786440 | tf_op jit(solution)/shard_map/ppermute | solution.py:436
  260.7 2.8 %collective-permute-start.12 = (bf16[320,1024]{1,0:T(8,128)(2,1)S(1)}, bf16[320,1024]{1,0:T(8,128)(2,1)S(1)}, u32[]{:S(2)}, u32[]{:S(2)}) collective-permute-start(bf16[320,1024]{1,0:T(8,128)(2,1)S(1)} %get-tuple-element.61.a_ref), channel_id=1, source_target_pairs={{0,1},{1,0},{2,3},{3,2},{4,5},{5,4},{6,7},{7,6},{8,9},{9,8},{10,11... | collective-permute-start | bytes 1966088 | tf_op jit(solution)/shard_map/ppermute | solution.py:436
  264.2 8.2 %collective-permute-start.13 = (bf16[160,640]{1,0:T(8,128)(2,1)S(1)}, bf16[160,640]{1,0:T(8,128)(2,1)S(1)}, u32[]{:S(2)}, u32[]{:S(2)}) collective-permute-start(bf16[160,640]{1,0:T(8,128)(2,1)S(1)} %get-tuple-element.67), channel_id=1, source_target_pairs={{0,2},{1,3},{2,4},{3,5},{4,6},{5,7},{6,0},{7,1},{8,10},{9,11},{10,... | collective-permute-start | bytes 614408 | tf_op jit(solution)/shard_map/ppermute | solution.py:436
  265.0 9.2 %collective-permute-start.17 = (bf16[160,640]{1,0:T(8,128)(2,1)S(1)}, bf16[160,640]{1,0:T(8,128)(2,1)S(1)}, u32[]{:S(2)}, u32[]{:S(2)}) collective-permute-start(bf16[160,640]{1,0:T(8,128)(2,1)S(1)} %get-tuple-element.71), channel_id=1, source_target_pairs={{0,6},{1,7},{2,0},{3,1},{4,2},{5,3},{6,4},{7,5},{8,14},{9,15},{10,... | collective-permute-start | bytes 614408 | tf_op jit(solution)/shard_map/ppermute | solution.py:436
  267.7 9.0 %collective-permute-start.15 = (bf16[160,640]{1,0:T(8,128)(2,1)S(1)}, bf16[160,640]{1,0:T(8,128)(2,1)S(1)}, u32[]{:S(2)}, u32[]{:S(2)}) collective-permute-start(bf16[160,640]{1,0:T(8,128)(2,1)S(1)} %get-tuple-element.68), channel_id=1, source_target_pairs={{0,2},{1,3},{2,4},{3,5},{4,6},{5,7},{6,0},{7,1},{8,10},{9,11},{10,... | collective-permute-start | bytes 614408 | tf_op jit(solution)/shard_map/ppermute | solution.py:436
  269.5 8.8 %collective-permute-start.16 = (bf16[160,640]{1,0:T(8,128)(2,1)S(1)}, bf16[160,640]{1,0:T(8,128)(2,1)S(1)}, u32[]{:S(2)}, u32[]{:S(2)}) collective-permute-start(bf16[160,640]{1,0:T(8,128)(2,1)S(1)} %get-tuple-element.69), channel_id=1, source_target_pairs={{0,6},{1,7},{2,0},{3,1},{4,2},{5,3},{6,4},{7,5},{8,14},{9,15},{10,... | collective-permute-start | bytes 614408 | tf_op jit(solution)/shard_map/ppermute | solution.py:436
  272.4 8.3 %collective-permute-start.14 = (bf16[160,640]{1,0:T(8,128)(2,1)S(1)}, bf16[160,640]{1,0:T(8,128)(2,1)S(1)}, u32[]{:S(2)}, u32[]{:S(2)}) collective-permute-start(bf16[160,640]{1,0:T(8,128)(2,1)S(1)} %add_convert_fusion.1), channel_id=1, source_target_pairs={{0,2},{1,3},{2,4},{3,5},{4,6},{5,7},{6,0},{7,1},{8,10},{9,11},{10,... | collective-permute-start | bytes 614408 | tf_op jit(solution)/shard_map/ppermute | solution.py:436
  274.2 7.9 %collective-permute-start.18 = (bf16[160,640]{1,0:T(8,128)(2,1)S(1)}, bf16[160,640]{1,0:T(8,128)(2,1)S(1)}, u32[]{:S(2)}, u32[]{:S(2)}) collective-permute-start(bf16[160,640]{1,0:T(8,128)(2,1)S(1)} %add_convert_fusion), channel_id=1, source_target_pairs={{0,6},{1,7},{2,0},{3,1},{4,2},{5,3},{6,4},{7,5},{8,14},{9,15},{10,... | collective-permute-start | bytes 614408 | tf_op jit(solution)/shard_map/ppermute | solution.py:436

commit v3 on v0

--- a/solution.py
+++ b/solution.py
@@ -222,17 +222,18 @@
     out_ref, mine_ref, theirs_ref, acc_ref, va_ref, run_ref, buf_ref, sem, sems = rest[-9:]
     far = rest[n_near + 3 : -9]
     width = mine_ref.shape[1] // NX
-    fetches = [pltpu.make_async_copy(received_ref, theirs_ref, sems.at[NX])]
+    fetches = []
     for k in range(NX):
         chip = (place_ref[2] + k) % NX
         first = pl.multiple_of((chip * 2 + place_ref[3]) * width, 128)
-        fetches.append(
-            pltpu.make_async_copy(
-                weight_ref.at[:, pl.ds(first, width)],
-                mine_ref.at[:, pl.ds(k * width, width)],
-                sems.at[k],
+        for i, (src, dst) in enumerate(((weight_ref, mine_ref), (received_ref, theirs_ref))):
+            fetches.append(
+                pltpu.make_async_copy(
+                    src.at[:, pl.ds(first, width)],
+                    dst.at[:, pl.ds(k * width, width)],
+                    sems.at[2 * k + i],
+                )
             )
-        )
     for fetch in fetches:
         fetch.start()
     chunks = [s.at[i] for s in near for i in range(s.shape[0])]
@@ -292,7 +293,7 @@
         out_shape=[jax.ShapeDtypeStruct((CHUNK + BRANCH_ROWS, GROUP * HEAD_SIZE), BF16), half, half],
         in_specs=[SMEM]
         + [VMEM] * (4 + len(near))
-        + [HBM, pl.BlockSpec(memory_space=pl.ANY)]
+        + [HBM, HBM]
         + [HBM] * len(far),
         out_specs=[VMEM] * 3,
         scratch_shapes=[
@@ -301,7 +302,7 @@
             pltpu.VMEM(m.shape, F32),
             pltpu.VMEM((2 * CHUNK, HEAD_SIZE), BF16),
             pltpu.SemaphoreType.DMA(()),
-            pltpu.SemaphoreType.DMA((NX + 1,)),
+            pltpu.SemaphoreType.DMA((2 * NX,)),
         ],
         compiler_params=pltpu.CompilerParams(vmem_limit_bytes=24 << 20),
         cost_estimate=pl.CostEstimate(
@@ -315,37 +316,9 @@
         *near,
         in_vmem(acc0),
         in_hbm(weight),
-        received,
+        in_hbm(received),
         *[in_hbm(a) for a in far],
     )
-
-
-def copy_kernel(place_ref, w_ref, o_ref):
-    del place_ref
-    o_ref[...] = w_ref[...]
-
-
-def columns_for_other(weight, place, width):
-    depth = weight.shape[0]
-    rows = depth // 4
-
-    def source(i, j, p):
-        return j, (p[2] + i) % NX * 2 + 1 - p[3]
-
-    return pl.pallas_call(
-        copy_kernel,
-        out_shape=jax.ShapeDtypeStruct((depth, NX * width), BF16),
-        grid_spec=pltpu.PrefetchScalarGridSpec(
-            num_scalar_prefetch=1,
-            grid=(NX, 4),
-            in_specs=[pl.BlockSpec((rows, width), source)],
-            out_specs=pl.BlockSpec((rows, width), lambda i, j, p: (j, i)),
-        ),
-        compiler_params=pltpu.CompilerParams(vmem_limit_bytes=8 << 20),
-        cost_estimate=pl.CostEstimate(
-            flops=0, bytes_accessed=4 * depth * NX * width, transcendentals=0
-        ),
-    )(place, in_hbm(weight))
 
 
 def own_kernel(a_ref, w_ref, o_ref):
@@ -439,10 +412,8 @@
     kv = pack(document_key, document_value)
     from_down = send(kv, y_shift(1))
     from_up = send(kv, y_shift(-1))
-    kv, weight = together(kv, out_weight)
-    for_other = columns_for_other(weight, place, width)
-    from_down, for_other = together(from_down, for_other)
     from_far = send(from_down, y_shift(1))
+    received = send(out_weight, core_swap(), "head")
     column = jnp.stack([kv, from_up, from_far, from_down])
     column, kv = together(column, kv)
     right = send(column, z_shift(1))
@@ -489,8 +460,6 @@
     acc = block(place, q, m, acc0, [column], (0,), first=1, alias=False)
     far, shifts = [column], [0]
 
-    column, for_other = together(column, for_other)
-    received = send(for_other, core_swap(), "head")
     for s in (1, 2, 3):
         right, left, acc = together(right, left, acc)
         if s < 3:

time: 295 us -> 284 us (0.963)
  Pallas kernels: 238 us -> 227 us
  waiting for transfers between devices: 28.8 us -> 24.3 us
  local copies, waits for them, and re-layouts: 0.79 us -> 4.66 us
    pallas_call x1 -> x0, Pallas kernels: 11.3 us -> none  [columns_for_other(): pl.pallas_call(copy_kernel, out_shape=jax.ShapeDtypeStruct((depth, NX * w...]
    ppermute x19, waiting for transfers between devices: 28.8 us -> 24.3 us  [send(): return lax.ppermute(a, axis, pairs)]
  transfers between devices with their start and end apart: 19 -> 19, of which waited for: 11 -> 12; matrix products, arithmetic and copies ran while one was open for 0% -> 1% of each run, Pallas kernels for 15% -> 12%
where the time goes in v3:
time: 284 us; the launch traced here: 281 us
  Pallas kernels  227 us (80%)
  waiting for transfers between devices  24.3 us (9%)
  starting transfers between devices  22.1 us (8%)
  local copies, waits for them, and re-layouts  4.66 us (2%)
    pallas_call x1, Pallas kernels, last_block(): pl.pallas_call(functools.partial(last_kernel, len(near), shifts), out_sha...  191 us
    ppermute x19, waiting for transfers between devices, send(): return lax.ppermute(a, axis, pairs)  24.3 us
    pallas_call x4, Pallas kernels, block(): pl.pallas_call(functools.partial(block_kernel, first, shifts), out_shape=...  23.6 us
    ppermute x19, starting transfers between devices, send(): return lax.ppermute(a, axis, pairs)  22.1 us
  transfers between devices with their start and end apart: 19, of which 12 were waited for; matrix products, arithmetic and copies ran while one was open for 1% of the time, Pallas kernels for 12%

profile of v3, /device:TPU:254, one launch (start us, length us, event | category | flops | bytes accessed | tf_op | source)
XLA Modules:
  0.0 280.5 jit_solution(1394544917079465190)
XLA Ops:
  0.6 0.1 collective-permute-start.11
  0.7 1.6 shard_map.113.kv_ref
  2.3 0.2 collective-permute-start.1
  2.6 1.8 collective-permute-start
  4.4 4.1 %collective-permute-done.1 = bf16[512,128]{1,0:T(8,128)(2,1)S(1)} collective-permute-done((bf16[512,128]{1,0:T(8,128)(2,1)}, bf16[512,128]{1,0:T(8,128)(2,1)S(1)}, u32[]{:S(2)}, u32[]{:S(2)}) %collective-permute-start.1) | collective-permute-done | bytes 131104 | tf_op jit(solution)/shard_map/ppermute | solution.py:406
  8.4 1.5 collective-permute-start.2
  9.9 0.7 pad.7.fk_ref
  10.7 0.7 pad.8.fv_ref
  11.4 0.9 reshape.22.bq_ref
  12.3 0.1 pad_add_fusion.place_ref
  12.4 0.0 collective-permute-done
  12.4 1.1 collective-permute-done.2
  13.5 1.0 pad_maximum_fusion.rest_0_.rest_5_
  14.5 0.0 copy-start
  14.5 1.1 collective-permute-start.4
  15.6 2.2 collective-permute-start.3
  17.8 0.9 copy-done.7
  18.8 0.7 copy-done.8
  19.4 4.9 %shard_map.114 = (bf16[10,256,128]{2,1,0:T(8,128)(2,1)S(1)}, f32[10,256,256]{2,1,0:T(8,128)S(1)}, f32[10,256,128]{2,1,0:T(8,128)S(1)}) custom-call(s32[16]{0:T(128)S(1)} %copy-done.8, bf16[256,1024]{1,0:T(8,128)(2,1)} %dq_hbm.1, bf16[64,1024]{1,0:T(8,128)(2,1)S(1)} %reshape.22.bq_ref, bf16[512,128]{1,0:T(8,128)(2,1)S(1)} %copy-done.7, ...), custom_call_target="tpu_custom_call" | custom-call | flops 4294967296 | bytes 8388608 | tf_op jit(solution)/shard_map/pallas_call | solution.py:428
  24.3 0.0 copy-done
  24.3 3.2 %shard_map.115.acc_in = f32[10,256,256]{2,1,0:T(8,128)S(1)} custom-call(s32[4]{0:T(128)S(1)} %pad_add_fusion.place_ref, bf16[10,256,128]{2,1,0:T(8,128)(2,1)S(1)} %get-tuple-element.33.q_ref, f32[10,256,128]{2,1,0:T(8,128)S(1)} %get-tuple-element.34.m_ref, f32[10,256,256]{2,1,0:T(8,128)S(1)} %get-tuple-element.36.acc_in.rest_2_, ...), custom_call_target="tpu_custom_call" | custom-call | flops 1509949440 | bytes 8388608 | tf_op jit(solution)/shard_map/pallas_call | solution.py:194
  27.5 1.0 collective-permute-done.4.rest_1_.rest_7_
  28.5 0.0 collective-permute-done.3.rest_0_.rest_6_
  28.5 3.0 %collective-permute-start.5 = (bf16[4,512,128]{2,1,0:T(8,128)(2,1)S(1)}, bf16[4,512,128]{2,1,0:T(8,128)(2,1)S(1)}, u32[]{:S(2)}, u32[]{:S(2)}) collective-permute-start(bf16[4,512,128]{2,1,0:T(8,128)(2,1)S(1)} %collective-permute-done.3.rest_0_.rest_6_), channel_id=1, source_target_pairs={{0,8},{8,16},{16,24},{24,32},{32,40},{40,48},{48,56},{56,0},{64,72... | collective-permute-start | bytes 1572872 | tf_op jit(solution)/shard_map/ppermute | solution.py:406
  31.4 0.2 collective-permute-start.6
  31.7 6.8 %shard_map.116.acc_in = f32[10,256,256]{2,1,0:T(8,128)S(1)} custom-call(s32[4]{0:T(128)S(1)} %pad_add_fusion.place_ref, bf16[10,256,128]{2,1,0:T(8,128)(2,1)S(1)} %get-tuple-element.33.q_ref, f32[10,256,128]{2,1,0:T(8,128)S(1)} %get-tuple-element.34.m_ref, f32[10,256,256]{2,1,0:T(8,128)S(1)} %shard_map.115.acc_in, ...), custom_call_target="tpu_custom_call", output_to_operand_aliasing={{}: (3, {})} | custom-call | flops 4026531840 | bytes 8388608 | tf_op jit(solution)/shard_map/pallas_call | solution.py:194
  38.5 0.0 copy-done.3
  38.5 0.0 copy-done.4
  38.5 1.9 collective-permute-done.5.rest_0_.rest_8_
  40.4 3.6 %collective-permute-done.6.rest_1_.rest_9_ = bf16[4,512,128]{2,1,0:T(8,128)(2,1)S(1)} collective-permute-done((bf16[4,512,128]{2,1,0:T(8,128)(2,1)S(1)}, bf16[4,512,128]{2,1,0:T(8,128)(2,1)S(1)}, u32[]{:S(2)}, u32[]{:S(2)}) %collective-permute-start.6) | collective-permute-done | bytes 524320 | tf_op jit(solution)/shard_map/ppermute | solution.py:406
  44.0 0.1 collective-permute-start.7
  44.2 1.9 collective-permute-start.8
  46.1 6.8 %shard_map.117.acc_in = f32[10,256,256]{2,1,0:T(8,128)S(1)} custom-call(s32[4]{0:T(128)S(1)} %pad_add_fusion.place_ref, bf16[10,256,128]{2,1,0:T(8,128)(2,1)S(1)} %get-tuple-element.33.q_ref, f32[10,256,128]{2,1,0:T(8,128)S(1)} %get-tuple-element.34.m_ref, f32[10,256,256]{2,1,0:T(8,128)S(1)} %shard_map.116.acc_in, ...), custom_call_target="tpu_custom_call", output_to_operand_aliasing={{}: (3, {})} | custom-call | flops 4026531840 | bytes 8388608 | tf_op jit(solution)/shard_map/pallas_call | solution.py:194
  52.9 1.7 collective-permute-done.7.rest_0_.rest_10_
  54.6 1.5 collective-permute-done.8.rest_1_.rest_11_
  56.2 1.8 collective-permute-start.10
  58.0 1.5 collective-permute-start.9
  59.5 6.8 %shard_map.118.acc_in = f32[10,256,256]{2,1,0:T(8,128)S(1)} custom-call(s32[4]{0:T(128)S(1)} %pad_add_fusion.place_ref, bf16[10,256,128]{2,1,0:T(8,128)(2,1)S(1)} %get-tuple-element.33.q_ref, f32[10,256,128]{2,1,0:T(8,128)S(1)} %get-tuple-element.34.m_ref, f32[10,256,256]{2,1,0:T(8,128)S(1)} %shard_map.117.acc_in, ...), custom_call_target="tpu_custom_call", output_to_operand_aliasing={{}: (3, {})} | custom-call | flops 4026531840 | bytes 8388608 | tf_op jit(solution)/shard_map/pallas_call | solution.py:194
  66.3 0.0 collective-permute-done.10.rest_1_
  66.3 0.0 collective-permute-done.9.rest_0_
  66.3 0.0 collective-permute-done.11.rest_4_
  66.4 191.0 %shard_map.119 = (bf16[320,1024]{1,0:T(8,128)(2,1)S(1)}, bf16[1024,2560]{1,0:T(8,128)(2,1)S(1)}, bf16[1024,2560]{1,0:T(8,128)(2,1)S(1)}) custom-call(s32[4]{0:T(128)S(1)} %pad_add_fusion.place_ref, bf16[10,256,128]{2,1,0:T(8,128)(2,1)S(1)} %get-tuple-element.33.q_ref, f32[10,256,128]{2,1,0:T(8,128)S(1)} %get-tuple-element.34.m_ref, ...), custom_call_target="tpu_custom_call" | custom-call | flops 2013265920 | bytes 8388608 | tf_op jit(solution)/shard_map/pallas_call | solution.py:291
  257.3 0.1 collective-permute-start.12
  257.4 2.7 shard_map.120.own_ref
  260.2 0.0 collective-permute-done.12.b_ref
  260.2 0.7 shard_map.123
  260.9 0.8 collective-permute-start.13
  261.6 1.5 collective-permute-start.17
  263.2 1.2 shard_map.122
  264.4 1.8 collective-permute-start.15
  266.1 0.3 collective-permute-start.16
  266.5 2.6 collective-permute-done.13
  269.0 0.1 add_convert_fusion.1
  269.1 1.8 collective-permute-start.14
  270.8 0.0 collective-permute-done.17
  270.8 0.1 add_convert_fusion
  270.9 0.4 collective-permute-start.18
  271.3 0.7 shard_map.121.o_ref
  272.0 1.4 collective-permute-done.15.b1
  273.4 1.6 collective-permute-done.16.c0
  275.0 2.4 collective-permute-done.14.b0
  277.4 1.4 collective-permute-done.18.c1
  278.8 0.8 shard_map.124
  279.7 0.7 reshape.27
  (14 shorter events, 0.1 us)
Async XLA Ops:
  0.6 65.7 %collective-permute-start.11 = (bf16[1024,5120]{1,0:T(8,128)(2,1)}, bf16[1024,5120]{1,0:T(8,128)(2,1)}, u32[]{:S(2)}, u32[]{:S(2)}) collective-permute-start(bf16[1024,5120]{1,0:T(8,128)(2,1)} %rest_3_.1), channel_id=1, source_target_pairs={{0,1},{1,0},{2,3},{3,2},{4,5},{5,4},{6,7},{7,6},{8,9},{9,8},{10,11... | collective-permute-start | bytes 31457288 | tf_op jit(solution)/shard_map/ppermute | solution.py:406
  2.3 6.1 %collective-permute-start.1 = (bf16[512,128]{1,0:T(8,128)(2,1)}, bf16[512,128]{1,0:T(8,128)(2,1)S(1)}, u32[]{:S(2)}, u32[]{:S(2)}) collective-permute-start(bf16[512,128]{1,0:T(8,128)(2,1)} %shard_map.113.kv_ref), channel_id=1, source_target_pairs={{0,64},{8,72},{16,80},{24,88},{32,96},{40,104},{48,112},{56,120},{... | collective-permute-start | bytes 393224 | tf_op jit(solution)/shard_map/ppermute | solution.py:406
  2.6 9.9 %collective-permute-start = (bf16[512,128]{1,0:T(8,128)(2,1)}, bf16[512,128]{1,0:T(8,128)(2,1)S(1)}, u32[]{:S(2)}, u32[]{:S(2)}) collective-permute-start(bf16[512,128]{1,0:T(8,128)(2,1)} %shard_map.113.kv_ref), channel_id=1, source_target_pairs={{0,192},{8,200},{16,208},{24,216},{32,224},{40,232},{48,240},{56,2... | collective-permute-start | bytes 393224 | tf_op jit(solution)/shard_map/ppermute | solution.py:406
  8.4 5.1 %collective-permute-start.2 = (bf16[512,128]{1,0:T(8,128)(2,1)S(1)}, bf16[512,128]{1,0:T(8,128)(2,1)S(1)}, u32[]{:S(2)}, u32[]{:S(2)}) collective-permute-start(bf16[512,128]{1,0:T(8,128)(2,1)S(1)} %collective-permute-done.1), channel_id=1, source_target_pairs={{0,64},{8,72},{16,80},{24,88},{32,96},{40,104},{48,112},{56,120},{... | collective-permute-start | bytes 393224 | tf_op jit(solution)/shard_map/ppermute | solution.py:406
  14.5 9.7 %copy-start = (bf16[4,512,128]{2,1,0:T(8,128)(2,1)}, bf16[4,512,128]{2,1,0:T(8,128)(2,1)S(1)}, u32[]{:S(2)}) copy-start(bf16[4,512,128]{2,1,0:T(8,128)(2,1)S(1)} %pad_maximum_fusion.rest_0_.rest_5_) | copy-start | bytes 1572868
  14.5 13.9 %collective-permute-start.4 = (bf16[4,512,128]{2,1,0:T(8,128)(2,1)S(1)}, bf16[4,512,128]{2,1,0:T(8,128)(2,1)S(1)}, u32[]{:S(2)}, u32[]{:S(2)}) collective-permute-start(bf16[4,512,128]{2,1,0:T(8,128)(2,1)S(1)} %pad_maximum_fusion.rest_0_.rest_5_), channel_id=1, source_target_pairs={{0,56},{8,0},{16,8},{24,16},{32,24},{40,32},{48,40},{56,48},{64,12... | collective-permute-start | bytes 1572872 | tf_op jit(solution)/shard_map/ppermute | solution.py:406
  15.6 12.9 %collective-permute-start.3 = (bf16[4,512,128]{2,1,0:T(8,128)(2,1)S(1)}, bf16[4,512,128]{2,1,0:T(8,128)(2,1)S(1)}, u32[]{:S(2)}, u32[]{:S(2)}) collective-permute-start(bf16[4,512,128]{2,1,0:T(8,128)(2,1)S(1)} %pad_maximum_fusion.rest_0_.rest_5_), channel_id=1, source_target_pairs={{0,8},{8,16},{16,24},{24,32},{32,40},{40,48},{48,56},{56,0},{64,72... | collective-permute-start | bytes 1572872 | tf_op jit(solution)/shard_map/ppermute | solution.py:406
  17.8 0.9 copy-start.7
  18.8 0.7 copy-start.8
  28.5 10.0 %copy-start.3 = (bf16[4,512,128]{2,1,0:T(8,128)(2,1)}, bf16[4,512,128]{2,1,0:T(8,128)(2,1)S(1)}, u32[]{:S(2)}) copy-start(bf16[4,512,128]{2,1,0:T(8,128)(2,1)S(1)} %collective-permute-done.4.rest_1_.rest_7_) | copy-start | bytes 1572868
  28.5 10.0 %copy-start.4 = (bf16[4,512,128]{2,1,0:T(8,128)(2,1)}, bf16[4,512,128]{2,1,0:T(8,128)(2,1)S(1)}, u32[]{:S(2)}) copy-start(bf16[4,512,128]{2,1,0:T(8,128)(2,1)S(1)} %collective-permute-done.3.rest_0_.rest_6_) | copy-start | bytes 1572868
  28.5 11.9 %collective-permute-start.5 = (bf16[4,512,128]{2,1,0:T(8,128)(2,1)S(1)}, bf16[4,512,128]{2,1,0:T(8,128)(2,1)S(1)}, u32[]{:S(2)}, u32[]{:S(2)}) collective-permute-start(bf16[4,512,128]{2,1,0:T(8,128)(2,1)S(1)} %collective-permute-done.3.rest_0_.rest_6_), channel_id=1, source_target_pairs={{0,8},{8,16},{16,24},{24,32},{32,40},{40,48},{48,56},{56,0},{64,72... | collective-permute-start | bytes 1572872 | tf_op jit(solution)/shard_map/ppermute | solution.py:406
  31.4 12.6 %collective-permute-start.6 = (bf16[4,512,128]{2,1,0:T(8,128)(2,1)S(1)}, bf16[4,512,128]{2,1,0:T(8,128)(2,1)S(1)}, u32[]{:S(2)}, u32[]{:S(2)}) collective-permute-start(bf16[4,512,128]{2,1,0:T(8,128)(2,1)S(1)} %collective-permute-done.4.rest_1_.rest_7_), channel_id=1, source_target_pairs={{0,56},{8,0},{16,8},{24,16},{32,24},{40,32},{48,40},{56,48},{64,12... | collective-permute-start | bytes 1572872 | tf_op jit(solution)/shard_map/ppermute | solution.py:406
  40.4 12.5 %copy-start.5 = (bf16[4,512,128]{2,1,0:T(8,128)(2,1)}, bf16[4,512,128]{2,1,0:T(8,128)(2,1)S(1)}, u32[]{:S(2)}) copy-start(bf16[4,512,128]{2,1,0:T(8,128)(2,1)S(1)} %collective-permute-done.5.rest_0_.rest_8_) | copy-start | bytes 1572868
  44.0 8.9 %copy-start.6 = (bf16[4,512,128]{2,1,0:T(8,128)(2,1)}, bf16[4,512,128]{2,1,0:T(8,128)(2,1)S(1)}, u32[]{:S(2)}) copy-start(bf16[4,512,128]{2,1,0:T(8,128)(2,1)S(1)} %collective-permute-done.6.rest_1_.rest_9_) | copy-start | bytes 1572868
  44.0 10.5 %collective-permute-start.7 = (bf16[4,512,128]{2,1,0:T(8,128)(2,1)S(1)}, bf16[4,512,128]{2,1,0:T(8,128)(2,1)S(1)}, u32[]{:S(2)}, u32[]{:S(2)}) collective-permute-start(bf16[4,512,128]{2,1,0:T(8,128)(2,1)S(1)} %collective-permute-done.5.rest_0_.rest_8_), channel_id=1, source_target_pairs={{0,8},{8,16},{16,24},{24,32},{32,40},{40,48},{48,56},{56,0},{64,72... | collective-permute-start | bytes 1572872 | tf_op jit(solution)/shard_map/ppermute | solution.py:406
  44.2 12.0 %collective-permute-start.8 = (bf16[4,512,128]{2,1,0:T(8,128)(2,1)S(1)}, bf16[4,512,128]{2,1,0:T(8,128)(2,1)S(1)}, u32[]{:S(2)}, u32[]{:S(2)}) collective-permute-start(bf16[4,512,128]{2,1,0:T(8,128)(2,1)S(1)} %collective-permute-done.6.rest_1_.rest_9_), channel_id=1, source_target_pairs={{0,56},{8,0},{16,8},{24,16},{32,24},{40,32},{48,40},{56,48},{64,12... | collective-permute-start | bytes 1572872 | tf_op jit(solution)/shard_map/ppermute | solution.py:406
  54.6 11.7 %copy-start.1 = (bf16[4,512,128]{2,1,0:T(8,128)(2,1)}, bf16[4,512,128]{2,1,0:T(8,128)(2,1)S(1)}, u32[]{:S(2)}) copy-start(bf16[4,512,128]{2,1,0:T(8,128)(2,1)S(1)} %collective-permute-done.7.rest_0_.rest_10_) | copy-start | bytes 1572868
  56.1 10.2 %copy-start.2 = (bf16[4,512,128]{2,1,0:T(8,128)(2,1)}, bf16[4,512,128]{2,1,0:T(8,128)(2,1)S(1)}, u32[]{:S(2)}) copy-start(bf16[4,512,128]{2,1,0:T(8,128)(2,1)S(1)} %collective-permute-done.8.rest_1_.rest_11_) | copy-start | bytes 1572868
  56.2 10.2 %collective-permute-start.10 = (bf16[2,512,128]{2,1,0:T(8,128)(2,1)S(1)}, bf16[2,512,128]{2,1,0:T(8,128)(2,1)S(1)}, u32[]{:S(2)}, u32[]{:S(2)}) collective-permute-start(bf16[2,512,128]{2,1,0:T(8,128)(2,1)S(1)} %slice.7), channel_id=1, source_target_pairs={{0,56},{8,0},{16,8},{24,16},{32,24},{40,32},{48,40},{56,48},{64,12... | collective-permute-start | bytes 786440 | tf_op jit(solution)/shard_map/ppermute | solution.py:406
  58.0 8.3 %collective-permute-start.9 = (bf16[2,512,128]{2,1,0:T(8,128)(2,1)S(1)}, bf16[2,512,128]{2,1,0:T(8,128)(2,1)S(1)}, u32[]{:S(2)}, u32[]{:S(2)}) collective-permute-start(bf16[2,512,128]{2,1,0:T(8,128)(2,1)S(1)} %slice.6), channel_id=1, source_target_pairs={{0,8},{8,16},{16,24},{24,32},{32,40},{40,48},{48,56},{56,0},{64,72... | collective-permute-start | bytes 786440 | tf_op jit(solution)/shard_map/ppermute | solution.py:406
  257.3 2.8 %collective-permute-start.12 = (bf16[320,1024]{1,0:T(8,128)(2,1)S(1)}, bf16[320,1024]{1,0:T(8,128)(2,1)S(1)}, u32[]{:S(2)}, u32[]{:S(2)}) collective-permute-start(bf16[320,1024]{1,0:T(8,128)(2,1)S(1)} %get-tuple-element.49.a_ref), channel_id=1, source_target_pairs={{0,1},{1,0},{2,3},{3,2},{4,5},{5,4},{6,7},{7,6},{8,9},{9,8},{10,11... | collective-permute-start | bytes 1966088 | tf_op jit(solution)/shard_map/ppermute | solution.py:406
  260.9 8.2 %collective-permute-start.13 = (bf16[160,640]{1,0:T(8,128)(2,1)S(1)}, bf16[160,640]{1,0:T(8,128)(2,1)S(1)}, u32[]{:S(2)}, u32[]{:S(2)}) collective-permute-start(bf16[160,640]{1,0:T(8,128)(2,1)S(1)} %get-tuple-element.55), channel_id=1, source_target_pairs={{0,2},{1,3},{2,4},{3,5},{4,6},{5,7},{6,0},{7,1},{8,10},{9,11},{10,... | collective-permute-start | bytes 614408 | tf_op jit(solution)/shard_map/ppermute | solution.py:406
  261.6 9.2 %collective-permute-start.17 = (bf16[160,640]{1,0:T(8,128)(2,1)S(1)}, bf16[160,640]{1,0:T(8,128)(2,1)S(1)}, u32[]{:S(2)}, u32[]{:S(2)}) collective-permute-start(bf16[160,640]{1,0:T(8,128)(2,1)S(1)} %get-tuple-element.59), channel_id=1, source_target_pairs={{0,6},{1,7},{2,0},{3,1},{4,2},{5,3},{6,4},{7,5},{8,14},{9,15},{10,... | collective-permute-start | bytes 614408 | tf_op jit(solution)/shard_map/ppermute | solution.py:406
  264.4 9.0 %collective-permute-start.15 = (bf16[160,640]{1,0:T(8,128)(2,1)S(1)}, bf16[160,640]{1,0:T(8,128)(2,1)S(1)}, u32[]{:S(2)}, u32[]{:S(2)}) collective-permute-start(bf16[160,640]{1,0:T(8,128)(2,1)S(1)} %get-tuple-element.56), channel_id=1, source_target_pairs={{0,2},{1,3},{2,4},{3,5},{4,6},{5,7},{6,0},{7,1},{8,10},{9,11},{10,... | collective-permute-start | bytes 614408 | tf_op jit(solution)/shard_map/ppermute | solution.py:406
  266.1 8.8 %collective-permute-start.16 = (bf16[160,640]{1,0:T(8,128)(2,1)S(1)}, bf16[160,640]{1,0:T(8,128)(2,1)S(1)}, u32[]{:S(2)}, u32[]{:S(2)}) collective-permute-start(bf16[160,640]{1,0:T(8,128)(2,1)S(1)} %get-tuple-element.57), channel_id=1, source_target_pairs={{0,6},{1,7},{2,0},{3,1},{4,2},{5,3},{6,4},{7,5},{8,14},{9,15},{10,... | collective-permute-start | bytes 614408 | tf_op jit(solution)/shard_map/ppermute | solution.py:406
  269.1 8.3 %collective-permute-start.14 = (bf16[160,640]{1,0:T(8,128)(2,1)S(1)}, bf16[160,640]{1,0:T(8,128)(2,1)S(1)}, u32[]{:S(2)}, u32[]{:S(2)}) collective-permute-start(bf16[160,640]{1,0:T(8,128)(2,1)S(1)} %add_convert_fusion.1), channel_id=1, source_target_pairs={{0,2},{1,3},{2,4},{3,5},{4,6},{5,7},{6,0},{7,1},{8,10},{9,11},{10,... | collective-permute-start | bytes 614408 | tf_op jit(solution)/shard_map/ppermute | solution.py:406
  270.9 7.9 %collective-permute-start.18 = (bf16[160,640]{1,0:T(8,128)(2,1)S(1)}, bf16[160,640]{1,0:T(8,128)(2,1)S(1)}, u32[]{:S(2)}, u32[]{:S(2)}) collective-permute-start(bf16[160,640]{1,0:T(8,128)(2,1)S(1)} %add_convert_fusion), channel_id=1, source_target_pairs={{0,6},{1,7},{2,0},{3,1},{4,2},{5,3},{6,4},{7,5},{8,14},{9,15},{10,... | collective-permute-start | bytes 614408 | tf_op jit(solution)/shard_map/ppermute | solution.py:406
